TPU v7x, 128 devices: a whole 4x4x4 slice. The times are simulated.
128 devices in a mesh: dp: 32 (over y, x, z_lo), tensor: 4 (over z_hi, core).
Axes of the slice: x: 4, y: 4, z: 4 (z_hi: 2, z_lo: 2; z = z_hi * 2 + z_lo), core: 2. Of those that a mesh axis runs over, the one named last changes fastest.
Arguments:
- hidden_in: bfloat16 [32768, 1536], P(('dp', 'tensor')), may hold values from -6 to 6
- norm_gain: float32 [1536], replicated, may hold values from 0.1 to 1.9
- proj_zx: bfloat16 [1536, 2, 3072], P('dp', None, 'tensor'), may hold values from -0.15625 to 0.15625
- proj_shared: bfloat16 [1536, 256], P(('dp', 'tensor')), may hold values from -0.15625 to 0.15625
- proj_step: bfloat16 [1536, 48], P('dp', 'tensor'), may hold values from -0.15625 to 0.15625
- conv_inner: float32 [5, 3072], P(None, 'tensor'), may hold values from -0.5 to 0.5
- conv_shared: float32 [5, 256], replicated, may hold values from -0.5 to 0.5
- step_bias: float32 [48], P('tensor'), may hold values from -6 to -2
- decay_log: float32 [48], P('tensor'), may hold values from 0 to 2.7
- skip_gain: float32 [48], P('tensor'), may hold values from 0.5 to 1.5
- gated_gain: float32 [3072], P('tensor'), may hold values from 0.1 to 1.9
- proj_out: bfloat16 [3072, 1536], P('tensor', 'dp'), may hold values from -0.109375 to 0.109375
- out_grad: bfloat16 [32768, 1536], P(('dp', 'tensor')), may hold values from -6 to 6
- segments: int32 [32768], P('dp'), may hold values from 0 to 6, as said below
Outputs:
- hidden_out: bfloat16 [32768, 1536], P(('dp', 'tensor'))
- grad_hidden: bfloat16 [32768, 1536], P(('dp', 'tensor'))
- grad_norm_gain: float32 [1536], replicated
- grad_proj_zx: float32 [1536, 2, 3072], P('dp', None, 'tensor')
- grad_proj_shared: float32 [1536, 256], P(('dp', 'tensor'))
- grad_proj_step: float32 [1536, 48], P('dp', 'tensor')
- grad_conv_inner: float32 [5, 3072], P(None, 'tensor')
- grad_conv_shared: float32 [5, 256], replicated
- grad_step_bias: float32 [48], P('tensor')
- grad_decay_log: float32 [48], P('tensor')
- grad_skip_gain: float32 [48], P('tensor')
- grad_gated_gain: float32 [3072], P('tensor')
- grad_proj_out: float32 [3072, 1536], P('tensor', 'dp')
Inputs may be any that keep to these rules, and one draw needn't show every extreme that they name: `segments`: within each sequence of 1024 tokens the ids start at 0 and never fall; a document is a run of equal ids.
All inputs are finite; a program needn't handle non-finite values.
Results may differ from a plain program's by a relative error of at most 0.024.
Values may be sent and summed in bfloat16 or wider, within the bound.
No kernel may reach another device: no remote copies, remote signals or barrier semaphores. Data moves between devices by JAX's collectives and lax.ppermute only.
A program may use at most 256 MiB of HBM per device.

v0:
```python
import jax
import jax.numpy as jnp
from jax import lax
from jax.experimental import pallas as pl
from jax.experimental.pallas import tpu as pltpu
from jax.sharding import Mesh
from jax.sharding import PartitionSpec as P

EPS = 1e-05
DP = ("y", "x", "zl")
TENSOR = ("zh", "c")
SIZES = {"y": 4, "x": 4, "zl": 2, "zh": 2, "c": 2}

F32 = jnp.float32
BF16 = jnp.bfloat16
HIGH = lax.Precision.HIGHEST
FORWARD_BLOCK = 128
BACKWARD_BLOCK = 256
VMEM = 56 * 1024 * 1024
PARAMS = pltpu.CompilerParams(vmem_limit_bytes=VMEM)
NT = (((1,), (1,)), ((), ()))
TN = (((0,), (0,)), ((), ()))
VMEM_SPEC = pl.BlockSpec(memory_space=pltpu.VMEM)


def cost(us):
    return pl.CostEstimate(flops=int(us * 1e6), transcendentals=0, bytes_accessed=int(us * 3e3))


def whole(shape):
    return pl.BlockSpec(shape, lambda *i: (0,) * len(shape))


def column_block(rows, width, index):
    return pl.BlockSpec((rows, width), lambda *i: (0, index))


def first_specs(rows):
    return [column_block(rows, 384, index) for index in (2, 3, 4)]


def out_specs_of(rows):
    return [column_block(rows, 384, index) for index in (5, 6)]


def dot(a, b):
    return jnp.dot(a, b, preferred_element_type=F32)


def dot_nt(a, b):
    return lax.dot_general(a, b, NT, preferred_element_type=F32)


def sigmoid(a):
    return 0.5 * jnp.tanh(0.5 * a) + 0.5


def softplus(a):
    return jnp.maximum(a, 0.0) + jnp.log1p(jnp.exp(-jnp.abs(a)))


def conv_strip(ext, taps, aux, j):
    n = ext.shape[0] - 8
    lanes = slice(j * 128, (j + 1) * 128)
    total = taps[4:5, lanes] + taps[3:4, lanes] * ext[8 : 8 + n, lanes]
    for back in (1, 2, 3):
        total += taps[3 - back : 4 - back, lanes] * (
            aux[:, back - 1 : back] * ext[8 - back : 8 - back + n, lanes]
        )
    return total


def two_parts(value):
    high = value.astype(BF16)
    return jnp.concatenate([high, (value - high.astype(F32)).astype(BF16)], 1)


def spread_heads(cols, table):
    return dot(two_parts(cols), table)


def scan_forward_kernel(tok, rows, gate_w, out_a, out_b, weights_a, weights_b, weights_c, taps, heads, chan, gain, spread, aux, segrow, pre_out, scan_low, state_out, gate_low, mixed_low, sums_out, ext, act, carry, fed, scan_out, gate_out, mixed_out):
    n = tok.shape[0]
    pairs = carry.shape[1] // 128

    @pl.when(pl.program_id(0) == 0)
    def _():
        carry[...] = jnp.zeros_like(carry)
        ext[0:8, :] = jnp.zeros((8, ext.shape[1]), F32)

    pre = jnp.concatenate([dot(tok[...], w[...]) for w in (weights_a, weights_b, weights_c)], 1)
    pre_out[...] = pre
    wide = ext.shape[1]
    ext[8:, :] = pre[:, :wide]
    marks = aux[...]
    for j in range(wide // 128):
        total = conv_strip(ext, taps, marks, j)
        act[:, j * 128 : (j + 1) * 128] = total * sigmoid(total)
    ext[0:8, :] = ext[n : n + 8, :]

    step = softplus(pre[:, wide:] + heads[0:1, :])
    log_step = -step * heads[1:2, :]
    row = lax.broadcasted_iota(jnp.int32, (n, n), 0)
    col = lax.broadcasted_iota(jnp.int32, (n, n), 1)
    lower = (row >= col).astype(F32)
    cum = jnp.dot(lower, log_step, precision=HIGH, preferred_element_type=F32)
    cum_t = cum.T
    write = act[:, pairs * 128 : (pairs + 1) * 128]
    read = act[:, (pairs + 1) * 128 : (pairs + 2) * 128].astype(BF16)
    write_t = write.T.astype(BF16)
    allowed = (row >= col) & (marks[:, 8:9] == segrow[0:1, :])
    inner = jnp.where(allowed, dot(read, write_t), 0.0)
    last = cum[n - 1 : n, :]
    enters = jnp.exp(cum) * marks[:, 3:4]
    to_end = jnp.exp(last - cum) * marks[:, 4:5]
    keep = jnp.exp(last) * marks[n - 1 : n, 3:4]
    wide_cols = spread_heads(jnp.concatenate([step, enters, to_end, jnp.broadcast_to(keep, (8, 128))], 0), spread[...])
    held = carry[...]
    held_low = held.astype(BF16)
    state_out[0] = held_low
    from_state = dot(read, held_low)
    low_half = lax.broadcasted_iota(jnp.int32, (1, 128), 1) < 64
    for j in range(pairs):
        lanes = slice(j * 128, (j + 1) * 128)
        x = act[:, lanes]
        xdt = x * wide_cols[:n, lanes]
        parts = []
        for h in (2 * j, 2 * j + 1):
            decay = jnp.exp(jnp.minimum(cum[:, h : h + 1] - cum_t[h : h + 1, :], 0.0))
            parts.append((decay * inner).astype(BF16))
        xdt_low = xdt.astype(BF16)
        zero = jnp.zeros_like(xdt_low)
        pair = jnp.concatenate([jnp.where(low_half, xdt_low, zero), jnp.where(low_half, zero, xdt_low)], 0)
        y = dot(jnp.concatenate(parts, 1), pair)
        if j % 2 == 0:
            block = slice(128 * j, 128 * j + 256)
            gate_out[:, block] = dot(tok[...], gate_w[:, block])
        else:
            spot = 256 * (j // 2)
            out_w = (out_a[:, 0:256], jnp.concatenate([out_a[:, 256:], out_b[:, :128]], 1), out_b[:, 128:])[j // 2]
            mixed_out[:, spot : spot + 256] = dot(rows[...], out_w)
        y += wide_cols[n : 2 * n, lanes] * from_state[:, lanes] + chan[0:1, lanes] * x
        scan_out[:, lanes] = y
        fed[:, lanes] = (xdt * wide_cols[2 * n : 3 * n, lanes]).astype(BF16)
        carry[:, lanes] = held[:, lanes] * wide_cols[3 * n : 3 * n + 1, lanes]
    carry[...] += dot(write_t, fed[...])

    gate_pre = gate_out[...]
    grad_mixed = mixed_out[...]
    scanned = scan_out[...]
    gate_low[...] = gate_pre.astype(BF16)
    mixed_low[...] = grad_mixed.astype(BF16)
    scan_low[...] = scanned.astype(BF16)
    gated = scanned * (gate_pre * sigmoid(gate_pre))
    square = jnp.sum(gated * gated, axis=1, keepdims=True)
    inner = jnp.sum(grad_mixed * gain[0:1, :] * gated, axis=1, keepdims=True)
    lane = lax.broadcasted_iota(jnp.int32, (1, 128), 1)
    cols = jnp.where(lane == 0, square, jnp.where(lane == 1, inner, 0.0))
    sums_out[...] = cols.T[0:8, :]


def small_rows(value):
    high = value.astype(BF16)
    return jnp.concatenate([high, (value - high.astype(F32)).astype(BF16)], 0)


def read_small(rows):
    return rows[:16, :].astype(F32) + rows[16:, :].astype(F32)


def scan_backward_kernel(me, pre, pre_before, taps, heads, chan, sums, spread, aux, segrow, grad, state, tok, grad_gate, weights, norm_gain, gain_sums, *rest):
    row_outs, outs_a, outs_b = rest[:4], rest[4:8], rest[8:12]
    ext, gext, act, slope, carry, fed, back, rows, low_out, taps_out, heads_out, gains, all_tok, all_low, split, packed = rest[12:]
    n = pre.shape[0]
    pairs = carry.shape[1] // 128
    wide = ext.shape[1]
    gate_width = grad_gate.shape[1]

    @pl.when(pl.program_id(0) == 0)
    def _():
        carry[...] = jnp.zeros_like(carry)
        gext[n:, :] = jnp.zeros((8, wide), F32)
        taps_out[...] = jnp.zeros_like(taps_out)
        heads_out[...] = jnp.zeros_like(heads_out)
        rows[...] = jnp.zeros_like(rows)
        gains[...] = jnp.zeros_like(gains)

    marks = aux[...]
    ext[0:8, :] = pre_before[:, :wide]
    ext[8:, :] = pre[:, :wide]
    for j in range(wide // 128):
        lanes = slice(j * 128, (j + 1) * 128)
        total = conv_strip(ext, taps, marks, j)
        sig = sigmoid(total)
        value = total * sig
        act[:, lanes] = value
        slope[:, lanes] = sig + value * (1.0 - sig)

    step_arg = pre[:, wide:] + heads[0:1, :]
    step = softplus(step_arg)
    rate = heads[1:2, :]
    row = lax.broadcasted_iota(jnp.int32, (n, n), 0)
    col = lax.broadcasted_iota(jnp.int32, (n, n), 1)
    lower = (row >= col).astype(F32)
    cum = jnp.dot(lower, -step * rate, precision=HIGH, preferred_element_type=F32)
    cum_t = cum.T
    write = act[:, pairs * 128 : (pairs + 1) * 128]
    read = act[:, (pairs + 1) * 128 : (pairs + 2) * 128]
    read_t = read.T.astype(BF16)
    write_low = write.astype(BF16)
    read_low = read.astype(BF16)
    allowed = (row <= col) & (marks[:, 8:9] == segrow[0:1, :])
    inner_t = jnp.where(allowed, dot(write_low, read_t), 0.0)
    last = cum[n - 1 : n, :]
    enters = jnp.exp(cum) * marks[:, 9:10]
    to_end = jnp.exp(last - cum) * marks[:, 10:11]
    keep = jnp.exp(last) * marks[n - 1 : n, 9:10]
    wide_cols = spread_heads(jnp.concatenate([step, enters, to_end, jnp.broadcast_to(keep, (8, 128))], 0), spread[...])
    held = state[0]
    later = carry[...]
    later_low = later.astype(BF16)
    from_state = dot(read_low, held)
    from_later = dot(write_low, later_low)
    low_half = lax.broadcasted_iota(jnp.int32, (1, 128), 1) < 64
    head_lane = lax.broadcasted_iota(jnp.int32, (1, 128), 1)
    grad_inner = jnp.zeros((n, n), F32)
    col_sums = jnp.zeros((n, 128), F32)
    to_end_part = jnp.zeros((n, 128), F32)
    enter_part = jnp.zeros((n, 128), F32)
    step_part = jnp.zeros((n, 128), F32)
    skip_part = jnp.zeros((n, 128), F32)
    keep_part = jnp.zeros((8, 128), F32)

    def head_sums(value, j):
        return dot(two_parts(value), sums[j])

    for j in range(pairs):
        lanes = slice(j * 128, (j + 1) * 128)
        x = act[:, lanes]
        dy = grad[:, lanes].astype(F32)
        step_wide = wide_cols[:n, lanes]
        xdt = x * step_wide
        xdt_low = xdt.astype(BF16)
        dy_low = dy.astype(BF16)
        zero = jnp.zeros_like(xdt_low)
        products = dot_nt(
            jnp.concatenate([jnp.where(low_half, xdt_low, zero), jnp.where(low_half, zero, xdt_low)], 0),
            dy_low,
        )
        parts = []
        for k, h in enumerate((2 * j, 2 * j + 1)):
            product = products[k * n : (k + 1) * n, :]
            decay = jnp.exp(jnp.minimum(cum_t[h : h + 1, :] - cum[:, h : h + 1], 0.0))
            scaled = decay * product
            grad_inner += scaled
            weighted = scaled * inner_t
            rows[h : h + 1, :] = jnp.sum(weighted, axis=0, keepdims=True)
            col_sums += jnp.where(head_lane == h, jnp.sum(weighted, axis=1, keepdims=True), 0.0)
            parts.append((decay * inner_t).astype(BF16))
        grad_pair = jnp.concatenate([jnp.where(low_half, dy_low, zero), jnp.where(low_half, zero, dy_low)], 0)
        grad_xdt = dot(jnp.concatenate(parts, 1), grad_pair)
        end_wide = wide_cols[2 * n : 3 * n, lanes]
        enter_wide = wide_cols[n : 2 * n, lanes]
        later_part = end_wide * from_later[:, lanes]
        grad_xdt += later_part
        to_end_part += head_sums(later_part * xdt, j)
        fed[:, lanes] = (xdt * end_wide).astype(BF16)
        grad_enter = dy * enter_wide
        back[:, lanes] = grad_enter.astype(BF16)
        enter_part += head_sums(grad_enter * from_state[:, lanes], j)
        step_part += head_sums(grad_xdt * x, j)
        skip_part += head_sums(dy * x, j)
        kept = jnp.sum(held[:, lanes].astype(F32) * later[:, lanes], axis=0, keepdims=True)
        keep_part += head_sums(jnp.broadcast_to(kept, (8, 128)), j)
        act[:, lanes] = grad_xdt * step_wide + chan[0:1, lanes] * dy
        carry[:, lanes] = later[:, lanes] * wide_cols[3 * n : 3 * n + 1, lanes]

    grad_cum = rows[...].T - col_sums + enter_part - to_end_part
    grad_last = jnp.sum(to_end_part, axis=0, keepdims=True) + keep * keep_part[0:1, :]
    upper = (row <= col).astype(F32)
    grad_log = jnp.dot(upper, grad_cum, precision=HIGH, preferred_element_type=F32) + grad_last
    grad_step = (step_part - rate * grad_log) * sigmoid(step_arg)
    heads_out[0:1, :] += jnp.sum(grad_step, axis=0, keepdims=True)
    heads_out[1:2, :] += -rate * jnp.sum(step * grad_log, axis=0, keepdims=True)
    heads_out[2:3, :] += jnp.sum(skip_part, axis=0, keepdims=True)
    low_out[:, gate_width + wide :] = grad_step.astype(BF16)

    grad_inner = jnp.where(allowed, grad_inner, 0.0)
    act[:, pairs * 128 : (pairs + 1) * 128] = dot(grad_inner.astype(BF16), read_low) + dot_nt(fed[...], later_low)
    act[:, (pairs + 1) * 128 : (pairs + 2) * 128] = dot(grad_inner.T.astype(BF16), write_low) + dot_nt(back[...], held)
    carry[...] += dot(read_t, back[...])

    for j in range(wide // 128):
        lanes = slice(j * 128, (j + 1) * 128)
        grad_pre = act[:, lanes] * slope[:, lanes]
        gext[0:n, lanes] = grad_pre
        total = taps[3:4, lanes] * grad_pre
        taps_out[3:4, lanes] += jnp.sum(grad_pre * ext[8 : 8 + n, lanes], axis=0, keepdims=True)
        taps_out[4:5, lanes] += jnp.sum(grad_pre, axis=0, keepdims=True)
        for by in (1, 2, 3):
            total += taps[3 - by : 4 - by, lanes] * (marks[:, 4 + by : 5 + by] * gext[by : by + n, lanes])
            taps_out[3 - by : 4 - by, lanes] += jnp.sum(
                grad_pre * (marks[:, by - 1 : by] * ext[8 - by : 8 - by + n, lanes]), axis=0, keepdims=True
            )
        low_out[:, gate_width + j * 128 : gate_width + (j + 1) * 128] = total.astype(BF16)
    gext[n:, :] = gext[0:8, :]

    step_id = pl.program_id(0)
    low_out[:, : grad_gate.shape[1]] = grad_gate[...]
    token_grad = dot_nt(low_out[...], weights[...])
    gains[0:1, :] += jnp.sum(token_grad * tok[...].astype(F32), axis=0, keepdims=True)
    place = pl.ds(pl.multiple_of((3 - step_id) * n, n), n)
    all_tok[place, :] = tok[...]
    all_low[place, :] = low_out[:, grad_gate.shape[1] :]
    token_low = token_grad.astype(BF16)
    for k in range(4):

        @pl.when((me[0] ^ (3 - k)) == 3 - step_id)
        def _():
            row_outs[k][...] = token_low

    @pl.when(step_id == 3)
    def _():
        cut = outs_a[0].shape[2]
        deep = outs_a[0].shape[1]
        for k in range(4):
            first = pl.multiple_of(((me[1] + k) % 4) * (4 * deep), 128)
            grad_rows = lax.dot_general(
                all_tok[:, pl.ds(first, 4 * deep)], all_low[...], TN, preferred_element_type=F32
            ).astype(BF16)
            outs_a[k][...] = grad_rows[:, :cut].reshape(outs_a[k].shape)
            split[...] = grad_rows[:, cut:]
            y = (me[1] + k) % 4
            for d in range(4):
                start = pl.multiple_of(((me[2] + d) % 4) * deep, 16)
                outs_b[d][pl.ds(pl.multiple_of(y * deep, 16), deep), :] = split[pl.ds(start, deep), :]
        width = gain_sums.shape[1]
        by_gain = gains[0:1, :] / norm_gain[0:1, :]
        packed[0:5, :] = taps_out[0:5, :]
        packed[5:6, :width] = gain_sums[0:1, :]
        packed[5:6, width:] = jnp.zeros((1, 1024 - width), F32)
        packed[6:7, :] = by_gain[:, :1024]
        packed[7:8, :512] = by_gain[:, 1024:]
        for r in range(3):
            packed[7:8, 512 + 128 * r : 640 + 128 * r] = heads_out[r : r + 1, :]
        packed[7:8, 896:] = jnp.zeros((1, 128), F32)
        sums_low = small_rows(jnp.concatenate([packed[:, :512], packed[:, 512:]], 0))
        for k in range(4):
            outs_b[k][4 * deep :, :512] = sums_low
            outs_b[k][4 * deep :, 512:] = jnp.zeros((32, outs_b[k].shape[1] - 512), BF16)


def scan_marks(segments):
    length = segments.shape[0]

    def same(by):
        if by > 0:
            other = jnp.concatenate([jnp.full((by,), -1, jnp.int32), segments[:-by]], 0)
        else:
            other = jnp.concatenate([segments[-by:], jnp.full((-by,), -1, jnp.int32)], 0)
        return other == segments

    def ends(size):
        blocks = segments.reshape(-1, size)
        before = jnp.concatenate([jnp.full((1,), -1, jnp.int32), blocks[:-1, -1]], 0)
        return [(blocks == before[:, None]).reshape(-1), (blocks == blocks[:, -1:]).reshape(-1)]

    cols = [same(1), same(2), same(3), *ends(FORWARD_BLOCK)]
    cols += [same(-1), same(-2), same(-3), segments, *ends(BACKWARD_BLOCK)]
    marks = jnp.stack([c.astype(F32) for c in cols], 1)
    return jnp.pad(marks, ((0, 0), (0, 128 - len(cols)))), jnp.broadcast_to(segments.astype(F32), (8, length))


def scan_forward(tokens, grad_rows, weights, taps, heads, chan, gain, spread, marks, segrow):
    length, model = tokens.shape
    cols = 1152
    inner = cols - 384
    wide = cols - 128
    n = FORWARD_BLOCK
    blocks = length // n


    return pl.pallas_call(
        scan_forward_kernel,
        grid=(blocks,),
        in_specs=[
            pl.BlockSpec((n, model), lambda i: (i, 0)),
            pl.BlockSpec((n, model), lambda i: (i, 0)),
            column_block(model, inner, 0),
            *out_specs_of(model),
            *first_specs(model),
            whole((8, wide)),
            whole((8, 128)),
            whole((8, inner)),
            whole((8, inner)),
            whole((256, inner)),
            pl.BlockSpec((n, 128), lambda i: (i, 0)),
            pl.BlockSpec((8, n), lambda i: (0, i)),
        ],
        out_specs=[
            pl.BlockSpec((n, cols), lambda i: (i, 0)),
            pl.BlockSpec((n, inner), lambda i: (i, 0)),
            pl.BlockSpec((1, 128, inner), lambda i: (i, 0, 0)),
            pl.BlockSpec((n, inner), lambda i: (i, 0)),
            pl.BlockSpec((n, inner), lambda i: (i, 0)),
            pl.BlockSpec((8, n), lambda i: (0, i)),
        ],
        out_shape=[
            jax.ShapeDtypeStruct((length, cols), F32),
            jax.ShapeDtypeStruct((length, inner), BF16),
            jax.ShapeDtypeStruct((blocks, 128, inner), BF16),
            jax.ShapeDtypeStruct((length, inner), BF16),
            jax.ShapeDtypeStruct((length, inner), BF16),
            jax.ShapeDtypeStruct((8, length), F32),
        ],
        scratch_shapes=[
            pltpu.VMEM((n + 8, wide), F32),
            pltpu.VMEM((n, wide), F32),
            pltpu.VMEM((128, inner), F32),
            pltpu.VMEM((n, inner), BF16),
            pltpu.VMEM((n, inner), F32),
            pltpu.VMEM((n, inner), F32),
            pltpu.VMEM((n, inner), F32),
        ],
        compiler_params=PARAMS,
        cost_estimate=cost(20),
        name="scan_forward",
    )(tokens, grad_rows, weights, weights, weights, weights, weights, weights, taps, heads, chan, gain, spread, marks, segrow)


def scan_backward(pre, taps, heads, chan, sums, spread, marks, segrow, grad, states, tokens, grad_gate, weights, norm_gain, gain_sums, me):
    length, cols = pre.shape
    model = tokens.shape[1]
    inner = cols - 384
    wide = cols - 128
    n = BACKWARD_BLOCK
    blocks = length // n
    cut = 512
    shape_a, shape_b = (4, model // 16, cut), (model // 4 + 32, cols - cut)

    def rev(i):
        return blocks - 1 - i

    def rows(width):
        return pl.BlockSpec((n, width), lambda i, me: (rev(i), 0))

    return pl.pallas_call(
        scan_backward_kernel,
        grid_spec=pltpu.PrefetchScalarGridSpec(
            num_scalar_prefetch=1,
            grid=(blocks,),
            in_specs=[
                rows(cols),
                pl.BlockSpec((8, cols), lambda i, me: (jnp.maximum(rev(i) * (n // 8) - 1, 0), 0)),
                whole((8, wide)),
                whole((8, 128)),
                whole((8, inner)),
                whole((inner // 128, 256, 128)),
                whole((256, inner)),
                rows(128),
                pl.BlockSpec((8, n), lambda i, me: (0, rev(i))),
                rows(inner),
                pl.BlockSpec((1, 128, inner), lambda i, me: (rev(i) * (n // FORWARD_BLOCK), 0, 0)),
                rows(model),
                rows(inner),
                column_block(model, inner + cols, 0),
                whole(norm_gain.shape),
                whole(gain_sums.shape),
            ],
            out_specs=[whole((n, model))] * 4 + [whole(shape_a)] * 4 + [whole(shape_b)] * 4,
            scratch_shapes=[
                pltpu.VMEM((n + 8, wide), F32),
                pltpu.VMEM((n + 8, wide), F32),
                pltpu.VMEM((n, wide), F32),
                pltpu.VMEM((n, wide), F32),
                pltpu.VMEM((128, inner), F32),
                pltpu.VMEM((n, inner), BF16),
                pltpu.VMEM((n, inner), BF16),
                pltpu.VMEM((128, n), F32),
                pltpu.VMEM((n, inner + cols), BF16),
                pltpu.VMEM((8, wide), F32),
                pltpu.VMEM((8, 128), F32),
                pltpu.VMEM((8, model), F32),
                pltpu.VMEM((length, model), BF16),
                pltpu.VMEM((length, cols), BF16),
                pltpu.VMEM((model // 4, cols - cut), BF16),
                pltpu.VMEM((8, 1024), F32),
            ],
        ),
        out_shape=[jax.ShapeDtypeStruct((n, model), BF16)] * 4
        + [jax.ShapeDtypeStruct(shape_a, BF16)] * 4
        + [jax.ShapeDtypeStruct(shape_b, BF16)] * 4,
        compiler_params=PARAMS,
        cost_estimate=cost(30),
        name="scan_backward",
    )(me, pre, pre, taps, heads, chan, sums, spread, marks, segrow, grad, states, tokens, grad_gate, weights, norm_gain, gain_sums)


def spread_table(inner):
    head = jnp.arange(inner) // 64
    return (jnp.arange(256)[:, None] % 128 == head[None, :]).astype(BF16)


def head_sum_table(inner):
    pairs = inner // 128
    lane = jnp.arange(256) % 128
    head = 2 * jnp.arange(pairs)[:, None] + (lane >= 64)[None, :]
    return (head[:, :, None] == jnp.arange(128)[None, None, :]).astype(BF16)


def store_block(value, outs):
    for k, out in enumerate(outs):

        @pl.when(pl.program_id(0) == k)
        def _():
            out[...] = value


def mix_second_kernel(channels, me, sums, gate, grad_mixed_in, scanned_in, out_a, out_b, gain, tok, rows, grad_scan, grad_gate, gain_out, grads_out, *rest):
    outs, all_gate, all_mixed = rest[:4], rest[4], rest[5]
    step = pl.program_id(0)
    n, width = gate.shape

    @pl.when(step == 0)
    def _():
        gain_out[...] = jnp.zeros_like(gain_out)

    @pl.when(step < 4)
    def _():
        cols = jnp.concatenate([sums[...], jnp.zeros((120, n), F32)], 0).T
        scale = lax.rsqrt(cols[:, 0:1] / channels + EPS)
        pull = scale * scale * scale * (cols[:, 1:2] / channels)
        gate_pre = gate[...].astype(F32)
        grad_mixed = grad_mixed_in[...].astype(F32)
        scanned = scanned_in[...].astype(F32)
        sig = sigmoid(gate_pre)
        silu = gate_pre * sig
        gated = scanned * silu
        scaled = gated * scale
        mixed = (scaled * gain[0:1, :]).astype(BF16)
        place = pl.ds(pl.multiple_of((me[0] ^ (3 - step)) * n, n), n)
        all_mixed[place, :] = mixed
        gain_out[0:1, :] += jnp.sum(grad_mixed * scaled, axis=0, keepdims=True)
        grad_gated = scale * gain[0:1, :] * grad_mixed - gated * pull
        grad_scan[...] = (grad_gated * silu).astype(BF16)
        grad_gate_low = (grad_gated * scanned * (sig + silu * (1.0 - sig))).astype(BF16)
        grad_gate[...] = grad_gate_low
        all_gate[place, :] = grad_gate_low
        projected = dot_nt(mixed[:, :384], out_a[...]) + dot_nt(mixed[:, 384:], out_b[...])
        store_block(projected.astype(BF16), outs)

    @pl.when(step >= 4)
    def _():
        gate_part = lax.dot_general(tok[...], all_gate[...], TN, preferred_element_type=F32)
        out_part = lax.dot_general(rows[...], all_mixed[...], TN, preferred_element_type=F32)
        grads_out[:, :width] = gate_part.astype(BF16)
        grads_out[:, width:] = out_part.astype(BF16)


def mix_second(sums, gate, grad_mixed, scanned, second, gain, tokens, grad_rows, channels, spot):
    length, width = gate.shape
    model = second.shape[0]
    n = 256
    m = model // 4

    def token_block(i, me):
        return me[0] ^ (3 - jnp.minimum(i, 3))

    def rows(cols):
        return pl.BlockSpec((n, cols), lambda i, me: (token_block(i, me), 0))

    def cols():
        return pl.BlockSpec((length, m), lambda i, me: (0, jnp.maximum(i - 4, 0)))

    return pl.pallas_call(
        lambda *refs: mix_second_kernel(channels, *refs),
        grid_spec=pltpu.PrefetchScalarGridSpec(
            num_scalar_prefetch=1,
            grid=(8,),
            in_specs=[
                pl.BlockSpec((8, n), lambda i, me: (0, token_block(i, me))),
                rows(width),
                rows(width),
                rows(width),
                *out_specs_of(model),
                whole((8, width)),
                cols(),
                cols(),
            ],
            out_specs=[
                rows(width),
                rows(width),
                whole((8, width)),
                pl.BlockSpec((m, 2 * width), lambda i, me: (jnp.maximum(i - 4, 0), 0)),
            ]
            + [whole((n, model))] * 4,
            scratch_shapes=[pltpu.VMEM((length, width), BF16), pltpu.VMEM((length, width), BF16)],
        ),
        out_shape=[
            jax.ShapeDtypeStruct((length, width), BF16),
            jax.ShapeDtypeStruct((length, width), BF16),
            jax.ShapeDtypeStruct((8, width), F32),
            jax.ShapeDtypeStruct((model, 2 * width), BF16),
        ]
        + [jax.ShapeDtypeStruct((n, model), BF16)] * 4,
        compiler_params=PARAMS,
        cost_estimate=cost(11),
        name="mix_second",
    )(spot, sums, gate, grad_mixed, scanned, second, second, gain, tokens, grad_rows)


def four_sum(own, ahead, across, behind):
    return (own.astype(F32) + across.astype(F32)) + (ahead.astype(F32) + behind.astype(F32))


def add_split_kernel(me, *refs):
    parts_a, parts_b, outs_a, outs_b = refs[:4], refs[4:8], refs[8:12], refs[12:]
    deep = outs_a[0].shape[0]
    sums = small_rows(four_sum(*[read_small(part[4 * deep :, :512]) for part in parts_b]))
    for d in range(4):
        e = (me[0] + d) % 4
        outs_a[d][...] = four_sum(*[part[e] for part in parts_a]).astype(BF16)
        place = pl.ds(pl.multiple_of(((me[1] + d) % 4) * deep, 16), deep)
        outs_b[d][:deep, :] = four_sum(*[part[place, :] for part in parts_b]).astype(BF16)
        outs_b[d][deep:, :512] = sums
        outs_b[d][deep:, 512:] = jnp.zeros((32, outs_b[d].shape[1] - 512), BF16)


def add_split(parts_a, parts_b, me):
    deep, width_a = parts_a[0].shape[1:]
    width_b = parts_b[0].shape[1]
    outs = pl.pallas_call(
        add_split_kernel,
        in_specs=[pl.BlockSpec(memory_space=pltpu.SMEM)] + [VMEM_SPEC] * 8,
        out_specs=[VMEM_SPEC] * 8,
        out_shape=[jax.ShapeDtypeStruct((deep, width_a), BF16)] * 4 + [jax.ShapeDtypeStruct((deep + 32, width_b), BF16)] * 4,
        compiler_params=PARAMS,
        name="add_split",
    )(me, *parts_a, *parts_b)
    return outs[:4], outs[4:]


def add_halve_kernel(me, *refs):
    ins, (keep, sums, give, total) = refs[:8], refs[8:]
    rows, cut = ins[0].shape
    total[:, :cut] = four_sum(*[part[...] for part in ins[:4]])
    total[:, cut:] = four_sum(*[part[:rows, :] for part in ins[4:]])
    n = keep.shape[0]
    keep[...] = total[pl.ds(pl.multiple_of(me[0] * n, 16), n), :]
    give[:n, :] = total[pl.ds(pl.multiple_of((1 - me[0]) * n, 16), n), :].astype(BF16)
    low = small_rows(four_sum(*[read_small(part[rows:, :512]) for part in ins[4:]]))
    give[n:, :512] = low
    give[n:, 512:] = jnp.zeros((32, give.shape[1] - 512), BF16)
    sums[...] = read_small(low)


def add_halve(parts_a, parts_b, me):
    rows = parts_a[0].shape[0]
    width = parts_a[0].shape[1] + parts_b[0].shape[1]
    return pl.pallas_call(
        add_halve_kernel,
        in_specs=[pl.BlockSpec(memory_space=pltpu.SMEM)] + [VMEM_SPEC] * 8,
        out_specs=[VMEM_SPEC] * 3,
        out_shape=[
            jax.ShapeDtypeStruct((rows // 2, width), F32),
            jax.ShapeDtypeStruct((16, 512), F32),
            jax.ShapeDtypeStruct((rows // 2 + 32, width), BF16),
        ],
        scratch_shapes=[pltpu.VMEM((rows, width), F32)],
        compiler_params=PARAMS,
        name="add_halve",
    )(me, *parts_a, *parts_b)


def place_kernel(me, *refs):
    out = refs[-1]
    for k, part in enumerate(refs[:-1]):

        @pl.when(pl.program_id(0) == k)
        def _():
            out[...] = part[...].reshape(out.shape)


def place(parts, index, me, shape, block, name):
    return pl.pallas_call(
        place_kernel,
        grid_spec=pltpu.PrefetchScalarGridSpec(
            num_scalar_prefetch=1,
            grid=(len(parts),),
            in_specs=[whole(p.shape) for p in parts],
            out_specs=pl.BlockSpec(block, lambda i, me: index(i, me[0])),
        ),
        out_shape=jax.ShapeDtypeStruct(shape, parts[0].dtype),
        compiler_params=PARAMS,
        cost_estimate=cost(2),
        name=name,
    )(me, *parts)


def shift(value, axis, by):
    n = SIZES[axis]
    return lax.ppermute(value, axis, [(i, (i - by) % n) for i in range(n)])


def swap(value, axis):
    return shift(value, axis, 1)


def ring(value, axis):
    return [value, shift(value, axis, 1), shift(value, axis, 2), shift(value, axis, -1)]


def sends(blocks, axis):
    return [blocks[0], shift(blocks[1], axis, -1), shift(blocks[2], axis, 2), shift(blocks[3], axis, 1)]


def tensor_xor(value, by):
    return lax.ppermute(value, TENSOR, [(i, i ^ by) for i in range(4)])


def sum_ring(value, axis):
    own, ahead, across, behind = ring(value, axis)
    return (own + across) + (ahead + behind)


def sum_pair(value, axis):
    return value + swap(value, axis)


def after(value, *others):
    return lax.optimization_barrier((value,) + others)[0]


def index_of(axis):
    return lax.axis_index(axis).reshape(1).astype(jnp.int32)


def pair_kernel(me, main, other_main, side, other_side, out):
    cut, middle = 1536, side.shape[1]
    for k, (left, right) in enumerate(((main, side), (other_main, other_side))):

        @pl.when(pl.program_id(0) == k)
        def _():
            out[:, :cut] = left[:, :cut]
            out[:, cut : cut + middle] = right[...]
            out[:, cut + middle :] = left[:, cut:]


def pair_rows(main, side):
    rows = main.shape[0]
    width = main.shape[1] + side.shape[1]
    parts = [main, swap(main, "zl"), side, swap(side, "zl")]
    return pl.pallas_call(
        pair_kernel,
        grid_spec=pltpu.PrefetchScalarGridSpec(
            num_scalar_prefetch=1,
            grid=(2,),
            in_specs=[whole(p.shape) for p in parts],
            out_specs=pl.BlockSpec((rows, width), lambda i, me: ((me[0] + i) % 2, 0)),
        ),
        out_shape=jax.ShapeDtypeStruct((2 * rows, width), BF16),
        compiler_params=PARAMS,
        name="pair_rows",
    )(index_of("zl"), *parts)


def token_place(own, near, far, both, me):
    rows, width = own.shape
    return place([own, near, far, both], lambda i, me: (me ^ i, 0), me, (4 * rows, width), (rows, width), "place_tokens")


def per_device(
    hidden_in,
    norm_gain,
    proj_zx,
    proj_shared,
    proj_step,
    conv_inner,
    conv_shared,
    step_bias,
    decay_log,
    skip_gain,
    gated_gain,
    proj_out,
    out_grad,
    segments,
):
    model_width = hidden_in.shape[1]
    width = proj_zx.shape[2]
    heads = step_bias.shape[0]
    me = {axis: index_of(axis) for axis in DP + TENSOR}
    spot = 2 * me["zh"] + me["c"]

    shared_parts = [proj_shared] + [tensor_xor(proj_shared, by) for by in (1, 2, 3)]
    shared_rows = jnp.zeros((48, 256), BF16)
    for by, part in enumerate(shared_parts):
        shared_rows = lax.dynamic_update_slice(shared_rows, part, (((spot[0] ^ by) * 12), jnp.int32(0)))
    side_rows = jnp.concatenate([shared_rows, jnp.pad(proj_step, ((0, 0), (0, 128 - heads)))], 1)
    main_rows = jnp.concatenate([proj_zx[:, 0, :], proj_zx[:, 1, :], proj_out.T], 1)
    weights = lax.all_gather(pair_rows(main_rows, side_rows), ("y", "x"), axis=0, tiled=True)

    residual_in = hidden_in.astype(F32)
    scale_in = lax.rsqrt(jnp.mean(residual_in * residual_in, axis=-1, keepdims=True) + EPS)
    normed_low = (residual_in * scale_in * norm_gain).astype(BF16)
    normed_far = swap(normed_low, "zh")
    normed_near = swap(normed_low, "c")

    normed_both = swap(normed_far, "c")
    tokens = token_place(normed_low, normed_near, normed_far, normed_both, spot)
    grad_far = swap(after(out_grad, normed_far), "zh")
    grad_near = swap(after(out_grad, normed_far), "c")
    grad_both = swap(grad_far, "c")
    grad_rows = token_place(out_grad, grad_near, grad_far, grad_both, spot)

    pad = (0, 128 - heads)
    head_rows = jnp.stack([jnp.pad(step_bias, pad), jnp.pad(jnp.exp(decay_log), pad)], 0)
    head_rows = jnp.pad(head_rows, ((0, 6), (0, 0)))
    taps = jnp.pad(jnp.concatenate([conv_inner, conv_shared], 1), ((0, 3), (0, 0)))
    chan = jnp.broadcast_to(jnp.repeat(skip_gain, width // heads), (8, width))
    gain = jnp.broadcast_to(gated_gain, (8, width))
    norm_rows = jnp.broadcast_to(norm_gain, (8, model_width))
    marks, segrow = scan_marks(segments)
    spread = spread_table(width)
    sum_table = head_sum_table(width)
    tokens, grad_rows = lax.optimization_barrier((tokens, grad_rows))
    pre, scanned, states, gate_pre, grad_mixed, sums = scan_forward(
        tokens, grad_rows, weights, taps, head_rows, chan, gain, spread, marks, segrow
    )

    sums = sum_pair(sum_pair(sums, "c"), "zh")
    grad_scanned, gate_grad_low, gain_sums, second_total, *out_blocks = mix_second(
        sums, gate_pre, grad_mixed, scanned, weights, gain, tokens, grad_rows, 4 * width, spot
    )
    out_far = (out_blocks[1].astype(F32) + swap(out_blocks[0], "c").astype(F32)).astype(BF16)
    out_near = swap(out_blocks[2], "c")
    second_sum = lax.psum_scatter(second_total, ("y", "x"), scatter_dimension=0, tiled=True)
    out_far_got = swap(out_far, "zh")

    grad_scanned = after(grad_scanned, out_far, second_total)
    sent = scan_backward(
        pre,
        taps,
        head_rows,
        chan,
        sum_table,
        spread,
        marks,
        segrow,
        grad_scanned,
        states,
        tokens,
        gate_grad_low,
        weights,
        norm_rows,
        gain_sums,
        jnp.concatenate([spot, me["y"], me["x"]]),
    )
    row_blocks = [after(block, out_far_got, out_near) for block in sent[:4]]
    far_got = swap(row_blocks[0], "c")
    row_far = (row_blocks[1].astype(F32) + far_got.astype(F32)).astype(BF16)
    row_far_got = swap(row_far, "zh")
    parts_b = sends([after(block, row_far) for block in sent[8:]], "x")
    parts_a = sends([after(block, row_far) for block in sent[4:8]], "y")
    half_a, half_b = add_split(parts_a, parts_b, jnp.concatenate([me["x"], me["y"]]))
    near_got = swap(after(row_blocks[2], *half_a), "c")

    hidden_out = (
        residual_in + (out_blocks[3].astype(F32) + out_near.astype(F32) + out_far_got.astype(F32))
    ).astype(BF16)
    grad_normed = row_blocks[3].astype(F32) + near_got.astype(F32) + row_far_got.astype(F32)
    weighted = jnp.sum(grad_normed * norm_gain * residual_in, axis=-1, keepdims=True)
    grad_hidden = (
        out_grad.astype(F32)
        + scale_in * norm_gain * grad_normed
        - residual_in * scale_in**3 * weighted / model_width
    ).astype(BF16)
    parts_a = [after(part, row_far_got, second_sum) for part in sends(half_a, "x")]
    parts_b = [after(part, row_far_got, second_sum) for part in sends(half_b, "y")]
    first_keep, small, first_give = add_halve(parts_a, parts_b, me["zl"])
    first_got = swap(first_give, "zl")
    first_mine = first_keep + first_got[:48].astype(F32)
    small = small + read_small(first_got[48:, :512])
    second_pairs = second_sum.reshape(2, 48, 2 * width)
    second_keep = lax.dynamic_index_in_dim(second_pairs, me["zl"][0], 0, keepdims=False)
    second_mine = second_keep.astype(F32) + swap(
        lax.dynamic_index_in_dim(second_pairs, 1 - me["zl"][0], 0, keepdims=False), "zl"
    ).astype(F32)
    grad_proj_out = second_mine[:, width:].T
    grad_proj_zx = jnp.stack([second_mine[:, :width], first_mine[:, :width]], 1)
    grad_proj_step = first_mine[:, width + 256 : width + 256 + heads]

    def quarter(by):
        part = lax.dynamic_slice(first_mine, ((spot[0] ^ by) * 12, jnp.int32(width)), (12, 256))
        return jnp.concatenate([small, jnp.pad(part, ((0, 0), (0, 256)))], 0)

    summed = (quarter(0) + tensor_xor(quarter(1), 1)) + (tensor_xor(quarter(2), 2) + tensor_xor(quarter(3), 3))
    rest = width - 512
    return (
        hidden_out,
        grad_hidden,
        jnp.concatenate([summed[6], summed[14], summed[7]]),
        grad_proj_zx,
        summed[16:, :256],
        grad_proj_step,
        jnp.concatenate([small[:5], small[8:13, :rest]], 1),
        summed[8:13, rest:],
        small[15, :heads],
        small[15, 128 : 128 + heads],
        small[15, 256 : 256 + heads],
        jnp.concatenate([small[5], small[13, :rest]]),
        grad_proj_out,
    )


def solution(mesh):
    fine = Mesh(mesh.devices.reshape(4, 4, 2, 2, 2), DP + TENSOR)
    both = DP + TENSOR
    return jax.shard_map(
        per_device,
        mesh=fine,
        in_specs=(
            P(both, None),
            P(),
            P(DP, None, TENSOR),
            P(both, None),
            P(DP, TENSOR),
            P(None, TENSOR),
            P(),
            P(TENSOR),
            P(TENSOR),
            P(TENSOR),
            P(TENSOR),
            P(TENSOR, DP),
            P(both, None),
            P(DP),
        ),
        out_specs=(
            P(both, None),
            P(both, None),
            P(),
            P(DP, None, TENSOR),
            P(both, None),
            P(DP, TENSOR),
            P(None, TENSOR),
            P(),
            P(TENSOR),
            P(TENSOR),
            P(TENSOR),
            P(TENSOR),
            P(TENSOR, DP),
        ),
        check_vma=False,
    )
```

profile of v0, /device:TPU:24, one launch (start us, length us, event | category | flops | bytes accessed | tf_op | source)
XLA Modules:
  0.0 291.3 jit_solution(8765072415810851647)
XLA Ops:
  9.5 2.0 collective-permute-start.6
  11.5 3.6 %collective-permute-start.8 = (bf16[12,256]{1,0:T(8,128)(2,1)}, bf16[12,256]{1,0:T(8,128)(2,1)S(1)}, u32[]{:S(2)}, u32[]{:S(2)}) collective-permute-start(bf16[12,256]{1,0:T(8,128)(2,1)} %param.17), channel_id=1, source_target_pairs={{0,2},{1,3},{2,0},{3,1},{4,6},{5,7},{6,4},{7,5},{8,10},{9,11},{10,... | collective-permute-start | bytes 18440 | tf_op jit(solution)/shard_map/ppermute | solution.py:718
  16.5 4.0 %collective-permute-done.8 = bf16[12,256]{1,0:T(8,128)(2,1)S(1)} collective-permute-done((bf16[12,256]{1,0:T(8,128)(2,1)}, bf16[12,256]{1,0:T(8,128)(2,1)S(1)}, u32[]{:S(2)}, u32[]{:S(2)}) %collective-permute-start.8) | collective-permute-done | bytes 6176 | tf_op jit(solution)/shard_map/ppermute | solution.py:718
  20.9 3.9 %collective-permute-done.10.other_side = bf16[48,384]{1,0:T(8,128)(2,1)S(1)} collective-permute-done((bf16[48,384]{1,0:T(8,128)(2,1)S(1)}, bf16[48,384]{1,0:T(8,128)(2,1)S(1)}, u32[]{:S(2)}, u32[]{:S(2)}) %collective-permute-start.10) | collective-permute-done | bytes 36896 | tf_op jit(solution)/shard_map/ppermute | solution.py:702
  25.5 1.9 pair_rows.1
  29.3 18.6 %collective-permute-done.1.refs_2_ = bf16[256,1536]{1,0:T(8,128)(2,1)S(1)} collective-permute-done((bf16[256,1536]{1,0:T(8,128)(2,1)S(1)}, bf16[256,1536]{1,0:T(8,128)(2,1)S(1)}, u32[]{:S(2)}, u32[]{:S(2)}) %collective-permute-start.1) | collective-permute-done | bytes 786464 | tf_op jit(solution)/shard_map/ppermute | solution.py:702
  50.6 16.2 %collective-permute-done.4.refs_2_ = bf16[256,1536]{1,0:T(8,128)(2,1)} collective-permute-done((bf16[256,1536]{1,0:T(8,128)(2,1)S(1)}, bf16[256,1536]{1,0:T(8,128)(2,1)}, u32[]{:S(2)}, u32[]{:S(2)}) %collective-permute-start.4) | collective-permute-done | bytes 786464 | tf_op jit(solution)/shard_map/ppermute | solution.py:702
  69.8 4.1 %place_tokens.2.tok.refs_8_ = bf16[1024,1536]{1,0:T(8,128)(2,1)} custom-call(s32[1]{0:T(128)} %bitcast.me.refs_0_, bf16[256,1536]{1,0:T(8,128)(2,1)} %copy-done.1, bf16[256,1536]{1,0:T(8,128)(2,1)} %collective-permute-done.refs_1_, bf16[256,1536]{1,0:T(8,128)(2,1)} %copy-done.7, bf16[256,1536]{1,0:T(8,128)(2,1)} %copy-done.10), custom_call_target="tpu_custom_call" | custom-call | flops 2000000 | bytes 6000 | tf_op jit(solution)/shard_map/place_tokens/pallas_call | solution.py:685
  75.7 4.1 %place_tokens.3.rows.refs_9_ = bf16[1024,1536]{1,0:T(8,128)(2,1)} custom-call(s32[1]{0:T(128)} %bitcast.me.refs_0_, bf16[256,1536]{1,0:T(8,128)(2,1)} %refs_0_.1, bf16[256,1536]{1,0:T(8,128)(2,1)} %copy-done.8, bf16[256,1536]{1,0:T(8,128)(2,1)} %collective-permute-done.4.refs_2_, bf16[256,1536]{1,0:T(8,128)(2,1)} %copy-done.9), custom_call_target="tpu_custom_call" | custom-call | flops 2000000 | bytes 6000 | tf_op jit(solution)/shard_map/place_tokens/pallas_call | solution.py:685
  79.8 16.4 %all-gather.2.cloned.1.call-done.gate_w.out_a.out_b.weights_a.weights_b.weights_c.refs_5_.refs_6_.weights = bf16[1536,2688]{1,0:T(8,128)(2,1)} async-done(((bf16[96,2688]{1,0:T(8,128)(2,1)}), bf16[1536,2688]{1,0:T(8,128)(2,1)}) %all-gather.2.cloned.1.call-update) | async-done | bytes 8257552 | tf_op jit(solution)/shard_map/all_gather | solution.py:800
  98.0 24.1 %scan_forward.1 = (f32[1024,1152]{1,0:T(8,128)}, bf16[1024,768]{1,0:T(8,128)(2,1)}, bf16[8,128,768]{2,1,0:T(8,128)(2,1)}, bf16[1024,768]{1,0:T(8,128)(2,1)}, bf1...) custom-call(bf16[1024,1536]{1,0:T(8,128)(2,1)} %place_tokens.2.tok.refs_8_, bf16[1024,1536]{1,0:T(8,128)(2,1)} %place_tokens.3.rows.refs_9_, ...), custom_call_target="tpu_custom_call" | custom-call | flops 20000000 | bytes 60000 | tf_op jit(solution)/shard_map/scan_forward/pallas_call | solution.py:383
  122.2 1.4 collective-permute-done.11
  124.4 3.1 %collective-permute-start.12 = (f32[8,1024]{1,0:T(8,128)S(1)}, f32[8,1024]{1,0:T(8,128)S(1)}, u32[]{:S(2)}, u32[]{:S(2)}) collective-permute-start(f32[8,1024]{1,0:T(8,128)S(1)} %add.178), channel_id=1, source_target_pairs={{0,2},{2,0},{1,3},{3,1},{4,6},{6,4},{5,7},{7,5},{8,10},{10,8},{9,1... | collective-permute-start | bytes 98312 | tf_op jit(solution)/shard_map/ppermute | solution.py:702
  127.5 2.3 collective-permute-done.12
  130.4 18.9 %mix_second.1 = (bf16[1024,768]{1,0:T(8,128)(2,1)}, bf16[1024,768]{1,0:T(8,128)(2,1)}, f32[8,768]{1,0:T(8,128)}, bf16[1536,1536]{1,0:T(8,128)(2,1)}, bf16[256,15...) custom-call(s32[1]{0:T(128)} %bitcast.me.refs_0_, ...), custom_call_target="tpu_custom_call" | custom-call | flops 11000000 | bytes 33000 | tf_op jit(solution)/shard_map/mix_second/pallas_call | solution.py:575
  150.5 1.5 collective-permute-done.14
  152.2 3.4 %collective-permute-start.15 = (bf16[256,1536]{1,0:T(8,128)(2,1)S(1)}, bf16[256,1536]{1,0:T(8,128)(2,1)S(1)}, u32[]{:S(2)}, u32[]{:S(2)}) collective-permute-start(bf16[256,1536]{1,0:T(8,128)(2,1)S(1)} %add_convert_fusion.1), channel_id=1, source_target_pairs={{0,2},{2,0},{1,3},{3,1},{4,6},{6,4},{5,7},{7,5},{8,10},{10,8},{9,1... | collective-permute-start | bytes 2359304 | tf_op jit(solution)/shard_map/ppermute | solution.py:702
  157.9 43.4 %scan_backward.1 = (bf16[256,1536]{1,0:T(8,128)(2,1)}, bf16[256,1536]{1,0:T(8,128)(2,1)}, bf16[256,1536]{1,0:T(8,128)(2,1)}, bf16[256,1536]{1,0:T(8,128)(2,1)}, ...) custom-call(s32[3]{0:T(128)} %pad_add_fusion.2.me, ...), custom_call_target="tpu_custom_call" | custom-call | flops 30000000 | bytes 90000 | tf_op jit(solution)/shard_map/scan_backward/pallas_call | solution.py:447
  201.4 2.5 collective-permute-done.16
  203.9 2.2 add_convert_fusion
  209.9 2.7 collective-permute-start.18
  212.6 17.7 %collective-permute-done.19.refs_3_ = bf16[4,96,512]{2,1,0:T(8,128)(2,1)S(1)} collective-permute-done((bf16[4,96,512]{2,1,0:T(8,128)(2,1)}, bf16[4,96,512]{2,1,0:T(8,128)(2,1)S(1)}, u32[]{:S(2)}, u32[]{:S(2)}) %collective-permute-start.19) | collective-permute-done | bytes 393248 | tf_op jit(solution)/shard_map/ppermute | solution.py:702
  230.9 7.1 %collective-permute-done.17.refs_1_ = bf16[4,96,512]{2,1,0:T(8,128)(2,1)S(1)} collective-permute-done((bf16[4,96,512]{2,1,0:T(8,128)(2,1)S(1)}, bf16[4,96,512]{2,1,0:T(8,128)(2,1)S(1)}, u32[]{:S(2)}, u32[]{:S(2)}) %collective-permute-start.17) | collective-permute-done | bytes 393248 | tf_op jit(solution)/shard_map/ppermute | solution.py:702
  240.2 3.3 %add_split.1 = (bf16[96,512]{1,0:T(8,128)(2,1)}, bf16[96,512]{1,0:T(8,128)(2,1)}, bf16[96,512]{1,0:T(8,128)(2,1)}, bf16[96,512]{1,0:T(8,128)(2,1)}, bf16[128,640...) custom-call(s32[2]{0:T(128)} %pad_add_fusion.3.me, ...), custom_call_target="tpu_custom_call" | custom-call | tf_op jit(solution)/shard_map/add_split/pallas_call | solution.py:632
  246.2 2.6 collective-permute-done.24
  249.7 2.7 collective-permute-start.29
  252.4 1.7 fusion.8
  255.0 3.0 %collective-permute-done.30.refs_7_ = bf16[128,640]{1,0:T(8,128)(2,1)S(1)} collective-permute-done((bf16[128,640]{1,0:T(8,128)(2,1)}, bf16[128,640]{1,0:T(8,128)(2,1)S(1)}, u32[]{:S(2)}, u32[]{:S(2)}) %collective-permute-start.30) | collective-permute-done | bytes 163872 | tf_op jit(solution)/shard_map/ppermute | solution.py:702
  258.9 4.1 %fusion.7 = (bf16[256,1536]{1,0:T(8,128)(2,1)}, bf16[256,1536]{1,0:T(8,128)(2,1)}) fusion(bf16[256,1536]{1,0:T(8,128)(2,1)S(1)} %copy-done, bf16[256,1536]{1,0:T(8,128)(2,1)S(1)} %copy-done.3, bf16[256,1536]{1,0:T(8,128)(2,1)S(1)} %collective-permute-done.24, bf16[256,1536]{1,0:T(8,128)(2,1)} %copy-done.5, bf16[256,1536]{1,0:T(8,128)(2,1)S(1)} %copy-done.4, ...), kind=kLoop, calls=%fused_computation.12 | loop fusion | flops 8650752 | bytes 7873536 | tf_op jit(solution)/shard_map/convert_element_type | solution.py:876
  264.2 2.2 add_halve.1
  267.9 4.3 %collective-permute-done.31 = bf16[80,1152]{1,0:T(8,128)(2,1)S(1)} collective-permute-done((bf16[80,1152]{1,0:T(8,128)(2,1)}, bf16[80,1152]{1,0:T(8,128)(2,1)S(1)}, u32[]{:S(2)}, u32[]{:S(2)}) %collective-permute-start.31) | collective-permute-done | bytes 184352 | tf_op jit(solution)/shard_map/ppermute | solution.py:702
  276.7 2.2 collective-permute-start.34
  (217 shorter events, 45.4 us)
Async XLA Ops:
  7.2 89.0 %all-gather.2.cloned.1.call-start = ((), (), s32[]{:S(2)}) async-start(), calls=%async_computation.1 | async-start | bytes 8773632 | tf_op jit(solution)/shard_map/all_gather | solution.py:800
  9.5 15.3 %collective-permute-start.6 = (bf16[48,2304]{1,0:T(8,128)(2,1)S(1)}, bf16[48,2304]{1,0:T(8,128)(2,1)S(1)}, u32[]{:S(2)}, u32[]{:S(2)}) collective-permute-start(bf16[48,2304]{1,0:T(8,128)(2,1)S(1)} %pad_maximum_fusion.1.main), channel_id=1, source_target_pairs={{0,4},{4,0},{1,5},{5,1},{2,6},{6,2},{3,7},{7,3},{8,12},{12,8},{9,1... | collective-permute-start | bytes 663560 | tf_op jit(solution)/shard_map/ppermute | solution.py:702
  11.5 9.0 %collective-permute-start.8 = (bf16[12,256]{1,0:T(8,128)(2,1)}, bf16[12,256]{1,0:T(8,128)(2,1)S(1)}, u32[]{:S(2)}, u32[]{:S(2)}) collective-permute-start(bf16[12,256]{1,0:T(8,128)(2,1)} %param.17), channel_id=1, source_target_pairs={{0,2},{1,3},{2,0},{3,1},{4,6},{5,7},{6,4},{7,5},{8,10},{9,11},{10,... | collective-permute-start | bytes 18440 | tf_op jit(solution)/shard_map/ppermute | solution.py:718
  15.1 5.5 %collective-permute-start.9 = (bf16[12,256]{1,0:T(8,128)(2,1)}, bf16[12,256]{1,0:T(8,128)(2,1)S(1)}, u32[]{:S(2)}, u32[]{:S(2)}) collective-permute-start(bf16[12,256]{1,0:T(8,128)(2,1)} %param.17), channel_id=1, source_target_pairs={{0,3},{1,2},{2,1},{3,0},{4,7},{5,6},{6,5},{7,4},{8,11},{9,10},{10,... | collective-permute-start | bytes 18440 | tf_op jit(solution)/shard_map/ppermute | solution.py:718
  27.5 226.6 %reduce-scatter.2.cloned.1.call-start = ((), (), s32[]{:S(2)}) async-start(), calls=%async_computation.2 | async-start | bytes 5013504 | tf_op jit(solution)/shard_map/reduce_scatter | solution.py:836
  28.1 19.8 %collective-permute-start.1 = (bf16[256,1536]{1,0:T(8,128)(2,1)S(1)}, bf16[256,1536]{1,0:T(8,128)(2,1)S(1)}, u32[]{:S(2)}, u32[]{:S(2)}) collective-permute-start(bf16[256,1536]{1,0:T(8,128)(2,1)S(1)} %fusion.2.refs_0_), channel_id=1, source_target_pairs={{0,2},{2,0},{1,3},{3,1},{4,6},{6,4},{5,7},{7,5},{8,10},{10,8},{9,1... | collective-permute-start | bytes 2359304 | tf_op jit(solution)/shard_map/ppermute | solution.py:702
  28.2 40.8 %collective-permute-start = (bf16[256,1536]{1,0:T(8,128)(2,1)S(1)}, bf16[256,1536]{1,0:T(8,128)(2,1)}, u32[]{:S(2)}, u32[]{:S(2)}) collective-permute-start(bf16[256,1536]{1,0:T(8,128)(2,1)S(1)} %fusion.2.refs_0_), channel_id=1, source_target_pairs={{0,1},{1,0},{2,3},{3,2},{4,5},{5,4},{6,7},{7,6},{8,9},{9,8},{10,11... | collective-permute-start | bytes 2359304 | tf_op jit(solution)/shard_map/ppermute | solution.py:702
  47.9 18.9 %collective-permute-start.4 = (bf16[256,1536]{1,0:T(8,128)(2,1)S(1)}, bf16[256,1536]{1,0:T(8,128)(2,1)}, u32[]{:S(2)}, u32[]{:S(2)}) collective-permute-start(bf16[256,1536]{1,0:T(8,128)(2,1)S(1)} %copy-done.2), channel_id=1, source_target_pairs={{0,2},{2,0},{1,3},{3,1},{4,6},{6,4},{5,7},{7,5},{8,10},{10,8},{9,1... | collective-permute-start | bytes 2359304 | tf_op jit(solution)/shard_map/ppermute | solution.py:702
  50.1 23.9 %collective-permute-start.3 = (bf16[256,1536]{1,0:T(8,128)(2,1)S(1)}, bf16[256,1536]{1,0:T(8,128)(2,1)S(1)}, u32[]{:S(2)}, u32[]{:S(2)}) collective-permute-start(bf16[256,1536]{1,0:T(8,128)(2,1)S(1)} %copy-done.2), channel_id=1, source_target_pairs={{0,1},{1,0},{2,3},{3,2},{4,5},{5,4},{6,7},{7,6},{8,9},{9,8},{10,11... | collective-permute-start | bytes 2359304 | tf_op jit(solution)/shard_map/ppermute | solution.py:702
  50.1 18.9 %collective-permute-start.2 = (bf16[256,1536]{1,0:T(8,128)(2,1)}, bf16[256,1536]{1,0:T(8,128)(2,1)S(1)}, u32[]{:S(2)}, u32[]{:S(2)}) collective-permute-start(bf16[256,1536]{1,0:T(8,128)(2,1)} %copy-done.7), channel_id=1, source_target_pairs={{0,1},{1,0},{2,3},{3,2},{4,5},{5,4},{6,7},{7,6},{8,9},{9,8},{10,11... | collective-permute-start | bytes 2359304 | tf_op jit(solution)/shard_map/ppermute | solution.py:702
  66.8 7.2 %collective-permute-start.5 = (bf16[256,1536]{1,0:T(8,128)(2,1)}, bf16[256,1536]{1,0:T(8,128)(2,1)S(1)}, u32[]{:S(2)}, u32[]{:S(2)}) collective-permute-start(bf16[256,1536]{1,0:T(8,128)(2,1)} %collective-permute-done.4.refs_2_), channel_id=1, source_target_pairs={{0,1},{1,0},{2,3},{3,2},{4,5},{5,4},{6,7},{7,6},{8,9},{9,8},{10,11... | collective-permute-start | bytes 2359304 | tf_op jit(solution)/shard_map/ppermute | solution.py:702
  124.4 5.4 %collective-permute-start.12 = (f32[8,1024]{1,0:T(8,128)S(1)}, f32[8,1024]{1,0:T(8,128)S(1)}, u32[]{:S(2)}, u32[]{:S(2)}) collective-permute-start(f32[8,1024]{1,0:T(8,128)S(1)} %add.178), channel_id=1, source_target_pairs={{0,2},{2,0},{1,3},{3,1},{4,6},{6,4},{5,7},{7,5},{8,10},{10,8},{9,1... | collective-permute-start | bytes 98312 | tf_op jit(solution)/shard_map/ppermute | solution.py:702
  150.5 50.8 %collective-permute-start.13 = (bf16[256,1536]{1,0:T(8,128)(2,1)S(1)}, bf16[256,1536]{1,0:T(8,128)(2,1)S(1)}, u32[]{:S(2)}, u32[]{:S(2)}) collective-permute-start(bf16[256,1536]{1,0:T(8,128)(2,1)S(1)} %copy-done.35), channel_id=1, source_target_pairs={{0,1},{1,0},{2,3},{3,2},{4,5},{5,4},{6,7},{7,6},{8,9},{9,8},{10,11... | collective-permute-start | bytes 2359304 | tf_op jit(solution)/shard_map/ppermute | solution.py:702
  152.2 49.2 %collective-permute-start.15 = (bf16[256,1536]{1,0:T(8,128)(2,1)S(1)}, bf16[256,1536]{1,0:T(8,128)(2,1)S(1)}, u32[]{:S(2)}, u32[]{:S(2)}) collective-permute-start(bf16[256,1536]{1,0:T(8,128)(2,1)S(1)} %add_convert_fusion.1), channel_id=1, source_target_pairs={{0,2},{2,0},{1,3},{3,1},{4,6},{6,4},{5,7},{7,5},{8,10},{10,8},{9,1... | collective-permute-start | bytes 2359304 | tf_op jit(solution)/shard_map/ppermute | solution.py:702
  206.1 24.1 %collective-permute-start.19 = (bf16[4,96,512]{2,1,0:T(8,128)(2,1)}, bf16[4,96,512]{2,1,0:T(8,128)(2,1)S(1)}, u32[]{:S(2)}, u32[]{:S(2)}) collective-permute-start(bf16[4,96,512]{2,1,0:T(8,128)(2,1)} %get-tuple-element.108), channel_id=1, source_target_pairs={{0,96},{32,0},{64,32},{96,64},{1,97},{33,1},{65,33},{97,65},{2,98}... | collective-permute-start | bytes 1179656 | tf_op jit(solution)/shard_map/ppermute | solution.py:702
  207.0 31.1 %collective-permute-start.22 = (bf16[416,640]{1,0:T(8,128)(2,1)S(1)}, bf16[416,640]{1,0:T(8,128)(2,1)S(1)}, u32[]{:S(2)}, u32[]{:S(2)}) collective-permute-start(bf16[416,640]{1,0:T(8,128)(2,1)S(1)} %copy-done.38), channel_id=1, source_target_pairs={{0,24},{8,0},{16,8},{24,16},{1,25},{9,1},{17,9},{25,17},{2,26},{10... | collective-permute-start | bytes 1597448 | tf_op jit(solution)/shard_map/ppermute | solution.py:702
  208.2 29.9 %collective-permute-start.21 = (bf16[416,640]{1,0:T(8,128)(2,1)S(1)}, bf16[416,640]{1,0:T(8,128)(2,1)S(1)}, u32[]{:S(2)}, u32[]{:S(2)}) collective-permute-start(bf16[416,640]{1,0:T(8,128)(2,1)S(1)} %copy-done.37), channel_id=1, source_target_pairs={{0,16},{8,24},{16,0},{24,8},{1,17},{9,25},{17,1},{25,9},{2,18},{10... | collective-permute-start | bytes 1597448 | tf_op jit(solution)/shard_map/ppermute | solution.py:702
  209.3 30.1 %collective-permute-start.20 = (bf16[416,640]{1,0:T(8,128)(2,1)S(1)}, bf16[416,640]{1,0:T(8,128)(2,1)S(1)}, u32[]{:S(2)}, u32[]{:S(2)}) collective-permute-start(bf16[416,640]{1,0:T(8,128)(2,1)S(1)} %copy-done.36), channel_id=1, source_target_pairs={{0,8},{8,16},{16,24},{24,0},{1,9},{9,17},{17,25},{25,1},{2,10},{10... | collective-permute-start | bytes 1597448 | tf_op jit(solution)/shard_map/ppermute | solution.py:702
  209.9 21.0 %collective-permute-start.18 = (bf16[4,96,512]{2,1,0:T(8,128)(2,1)}, bf16[4,96,512]{2,1,0:T(8,128)(2,1)S(1)}, u32[]{:S(2)}, u32[]{:S(2)}) collective-permute-start(bf16[4,96,512]{2,1,0:T(8,128)(2,1)} %get-tuple-element.106), channel_id=1, source_target_pairs={{0,64},{32,96},{64,0},{96,32},{1,65},{33,97},{65,1},{97,33},{2,66}... | collective-permute-start | bytes 1179656 | tf_op jit(solution)/shard_map/ppermute | solution.py:702
  230.3 7.8 %collective-permute-start.17 = (bf16[4,96,512]{2,1,0:T(8,128)(2,1)S(1)}, bf16[4,96,512]{2,1,0:T(8,128)(2,1)S(1)}, u32[]{:S(2)}, u32[]{:S(2)}) collective-permute-start(bf16[4,96,512]{2,1,0:T(8,128)(2,1)S(1)} %copy-done.39), channel_id=1, source_target_pairs={{0,32},{32,64},{64,96},{96,0},{1,33},{33,65},{65,97},{97,1},{2,34}... | collective-permute-start | bytes 1179656 | tf_op jit(solution)/shard_map/ppermute | solution.py:702
  230.9 17.9 %collective-permute-start.24 = (bf16[256,1536]{1,0:T(8,128)(2,1)}, bf16[256,1536]{1,0:T(8,128)(2,1)S(1)}, u32[]{:S(2)}, u32[]{:S(2)}) collective-permute-start(bf16[256,1536]{1,0:T(8,128)(2,1)} %add_convert_fusion), channel_id=1, source_target_pairs={{0,2},{2,0},{1,3},{3,1},{4,6},{6,4},{5,7},{7,5},{8,10},{10,8},{9,1... | collective-permute-start | bytes 2359304 | tf_op jit(solution)/shard_map/ppermute | solution.py:702
  243.6 20.0 %collective-permute-start.27 = (bf16[96,512]{1,0:T(8,128)(2,1)}, bf16[96,512]{1,0:T(8,128)(2,1)}, u32[]{:S(2)}, u32[]{:S(2)}) collective-permute-start(bf16[96,512]{1,0:T(8,128)(2,1)} %get-tuple-element.120), channel_id=1, source_target_pairs={{0,24},{8,0},{16,8},{24,16},{1,25},{9,1},{17,9},{25,17},{2,26},{10... | collective-permute-start | bytes 294920 | tf_op jit(solution)/shard_map/ppermute | solution.py:702
  244.7 18.8 %collective-permute-start.26 = (bf16[96,512]{1,0:T(8,128)(2,1)}, bf16[96,512]{1,0:T(8,128)(2,1)}, u32[]{:S(2)}, u32[]{:S(2)}) collective-permute-start(bf16[96,512]{1,0:T(8,128)(2,1)} %get-tuple-element.119), channel_id=1, source_target_pairs={{0,16},{8,24},{16,0},{24,8},{1,17},{9,25},{17,1},{25,9},{2,18},{10... | collective-permute-start | bytes 294920 | tf_op jit(solution)/shard_map/ppermute | solution.py:702
  245.4 18.2 %collective-permute-start.25 = (bf16[96,512]{1,0:T(8,128)(2,1)}, bf16[96,512]{1,0:T(8,128)(2,1)}, u32[]{:S(2)}, u32[]{:S(2)}) collective-permute-start(bf16[96,512]{1,0:T(8,128)(2,1)} %get-tuple-element.118), channel_id=1, source_target_pairs={{0,8},{8,16},{16,24},{24,0},{1,9},{9,17},{17,25},{25,1},{2,10},{10... | collective-permute-start | bytes 294920 | tf_op jit(solution)/shard_map/ppermute | solution.py:702
  248.8 9.2 %collective-permute-start.30 = (bf16[128,640]{1,0:T(8,128)(2,1)}, bf16[128,640]{1,0:T(8,128)(2,1)S(1)}, u32[]{:S(2)}, u32[]{:S(2)}) collective-permute-start(bf16[128,640]{1,0:T(8,128)(2,1)} %get-tuple-element.132), channel_id=1, source_target_pairs={{0,96},{32,0},{64,32},{96,64},{1,97},{33,1},{65,33},{97,65},{2,98}... | collective-permute-start | bytes 491528 | tf_op jit(solution)/shard_map/ppermute | solution.py:702
  249.7 8.3 %collective-permute-start.29 = (bf16[128,640]{1,0:T(8,128)(2,1)}, bf16[128,640]{1,0:T(8,128)(2,1)S(1)}, u32[]{:S(2)}, u32[]{:S(2)}) collective-permute-start(bf16[128,640]{1,0:T(8,128)(2,1)} %get-tuple-element.130), channel_id=1, source_target_pairs={{0,64},{32,96},{64,0},{96,32},{1,65},{33,97},{65,1},{97,33},{2,66}... | collective-permute-start | bytes 491528 | tf_op jit(solution)/shard_map/ppermute | solution.py:702
  258.0 5.5 %collective-permute-start.28 = (bf16[128,640]{1,0:T(8,128)(2,1)}, bf16[128,640]{1,0:T(8,128)(2,1)S(1)}, u32[]{:S(2)}, u32[]{:S(2)}) collective-permute-start(bf16[128,640]{1,0:T(8,128)(2,1)} %get-tuple-element.128), channel_id=1, source_target_pairs={{0,32},{32,64},{64,96},{96,0},{1,33},{33,65},{65,97},{97,1},{2,34}... | collective-permute-start | bytes 491528 | tf_op jit(solution)/shard_map/ppermute | solution.py:702
  258.0 9.1 %collective-permute-start.35 = (bf16[48,1536]{1,0:T(8,128)(2,1)S(1)}, bf16[48,1536]{1,0:T(8,128)(2,1)S(1)}, u32[]{:S(2)}, u32[]{:S(2)}) collective-permute-start(bf16[48,1536]{1,0:T(8,128)(2,1)S(1)} %dynamic-slice_bitcast_fusion), channel_id=1, source_target_pairs={{0,4},{4,0},{1,5},{5,1},{2,6},{6,2},{3,7},{7,3},{8,12},{12,8},{9,1... | collective-permute-start | bytes 442376 | tf_op jit(solution)/shard_map/ppermute | solution.py:702
  266.4 5.7 %collective-permute-start.31 = (bf16[80,1152]{1,0:T(8,128)(2,1)}, bf16[80,1152]{1,0:T(8,128)(2,1)S(1)}, u32[]{:S(2)}, u32[]{:S(2)}) collective-permute-start(bf16[80,1152]{1,0:T(8,128)(2,1)} %get-tuple-element.135), channel_id=1, source_target_pairs={{0,4},{4,0},{1,5},{5,1},{2,6},{6,2},{3,7},{7,3},{8,12},{12,8},{9,1... | collective-permute-start | bytes 552968 | tf_op jit(solution)/shard_map/ppermute | solution.py:702
  275.5 5.3 %collective-permute-start.32 = (f32[28,512]{1,0:T(8,128)S(1)}, f32[28,512]{1,0:T(8,128)S(1)}, u32[]{:S(2)}, u32[]{:S(2)}) collective-permute-start(f32[28,512]{1,0:T(8,128)S(1)} %get-tuple-element.206), channel_id=1, source_target_pairs={{0,1},{1,0},{2,3},{3,2},{4,5},{5,4},{6,7},{7,6},{8,9},{9,8},{10,11... | collective-permute-start | bytes 172040 | tf_op jit(solution)/shard_map/ppermute | solution.py:718
  275.6 6.4 %collective-permute-start.33 = (f32[28,512]{1,0:T(8,128)S(1)}, f32[28,512]{1,0:T(8,128)S(1)}, u32[]{:S(2)}, u32[]{:S(2)}) collective-permute-start(f32[28,512]{1,0:T(8,128)S(1)} %get-tuple-element.207), channel_id=1, source_target_pairs={{0,2},{1,3},{2,0},{3,1},{4,6},{5,7},{6,4},{7,5},{8,10},{9,11},{10,... | collective-permute-start | bytes 172040 | tf_op jit(solution)/shard_map/ppermute | solution.py:718
  276.7 5.9 %collective-permute-start.34 = (f32[28,512]{1,0:T(8,128)S(1)}, f32[28,512]{1,0:T(8,128)S(1)}, u32[]{:S(2)}, u32[]{:S(2)}) collective-permute-start(f32[28,512]{1,0:T(8,128)S(1)} %get-tuple-element.205), channel_id=1, source_target_pairs={{0,3},{1,2},{2,1},{3,0},{4,7},{5,6},{6,5},{7,4},{8,11},{9,10},{10,... | collective-permute-start | bytes 172040 | tf_op jit(solution)/shard_map/ppermute | solution.py:718
  (47 other events, 551.3 us)
Sparse Core Ops, SparseCore 0:
  27.6 68.6 all-gather.1
  149.5 88.3 reduce-scatter.1
where the time goes:
time: 296 us; the launch traced here: 291 us
  waiting for transfers between devices  105 us (35%)
  Pallas kernels  102 us (34%)
  starting transfers between devices  30.5 us (10%)
  local copies, waits for them, and re-layouts  19.6 us (7%)
  other arithmetic  19.3 us (7%)
  between operations  14.7 us (5%)
    ppermute x30, waiting for transfers between devices, shift(): return lax.ppermute(value, axis, [(i, (i - by) % n) for i in range(n)])  83 us
    pallas_call x1, Pallas kernels, scan_backward(): pl.pallas_call(scan_backward_kernel, grid_spec=pltpu.PrefetchScalarGridSp...  43.4 us
    pallas_call x1, Pallas kernels, scan_forward(): pl.pallas_call(scan_forward_kernel, grid=(blocks,), in_specs=[pl.BlockSpe...  24.1 us
    ppermute x30, starting transfers between devices, shift(): return lax.ppermute(value, axis, [(i, (i - by) % n) for i in range(n)])  23.2 us
    pallas_call x1, Pallas kernels, mix_second(): pl.pallas_call(lambda *refs: mix_second_kernel(channels, *refs), grid_spe...  18.9 us
    all_gather x1, waiting for transfers between devices, per_device(): lax.all_gather(pair_rows(main_rows, side_rows), ('y', 'x'), axis=0, tiled...  16.4 us
    unnamed x89, local copies, waits for them, and re-layouts  9.59 us
    pallas_call x2, Pallas kernels, place(): pl.pallas_call(place_kernel, grid_spec=pltpu.PrefetchScalarGridSpec(num_s...  8.24 us
  transfers between devices with their start and end apart: 38, of which 18 were waited for; matrix products, arithmetic and copies ran while one was open for 7% of the time, Pallas kernels for 20%

commit v1 on v0

--- a/solution.py
+++ b/solution.py
@@ -710,8 +710,10 @@
     return [value, shift(value, axis, 1), shift(value, axis, 2), shift(value, axis, -1)]
 
 
-def sends(blocks, axis):
-    return [blocks[0], shift(blocks[1], axis, -1), shift(blocks[2], axis, 2), shift(blocks[3], axis, 1)]
+def sends(blocks, axis, in_turn=False):
+    ahead, behind = shift(blocks[1], axis, -1), shift(blocks[3], axis, 1)
+    opposite = after(blocks[2], ahead, behind) if in_turn else blocks[2]
+    return [blocks[0], ahead, shift(opposite, axis, 2), behind]
 
 
 def tensor_xor(value, by):
@@ -810,7 +812,6 @@
     grad_far = swap(after(out_grad, normed_far), "zh")
     grad_near = swap(after(out_grad, normed_far), "c")
     grad_both = swap(grad_far, "c")
-    grad_rows = token_place(out_grad, grad_near, grad_far, grad_both, spot)
 
     pad = (0, 128 - heads)
     head_rows = jnp.stack([jnp.pad(step_bias, pad), jnp.pad(jnp.exp(decay_log), pad)], 0)
@@ -822,6 +823,10 @@
     marks, segrow = scan_marks(segments)
     spread = spread_table(width)
     sum_table = head_sum_table(width)
+    late, head_rows, taps, chan, gain, norm_rows, marks, segrow, spread, sum_table = lax.optimization_barrier(
+        (spot, head_rows, taps, chan, gain, norm_rows, marks, segrow, spread, sum_table)
+    )
+    grad_rows = token_place(out_grad, grad_near, grad_far, grad_both, late)
     tokens, grad_rows = lax.optimization_barrier((tokens, grad_rows))
     pre, scanned, states, gate_pre, grad_mixed, sums = scan_forward(
         tokens, grad_rows, weights, taps, head_rows, chan, gain, spread, marks, segrow
@@ -860,7 +865,7 @@
     row_far = (row_blocks[1].astype(F32) + far_got.astype(F32)).astype(BF16)
     row_far_got = swap(row_far, "zh")
     parts_b = sends([after(block, row_far) for block in sent[8:]], "x")
-    parts_a = sends([after(block, row_far) for block in sent[4:8]], "y")
+    parts_a = sends([after(block, row_far) for block in sent[4:8]], "y", in_turn=True)
     half_a, half_b = add_split(parts_a, parts_b, jnp.concatenate([me["x"], me["y"]]))
     near_got = swap(after(row_blocks[2], *half_a), "c")
 
@@ -875,7 +880,7 @@
         - residual_in * scale_in**3 * weighted / model_width
     ).astype(BF16)
     parts_a = [after(part, row_far_got, second_sum) for part in sends(half_a, "x")]
-    parts_b = [after(part, row_far_got, second_sum) for part in sends(half_b, "y")]
+    parts_b = [after(part, row_far_got, second_sum) for part in sends(half_b, "y", in_turn=True)]
     first_keep, small, first_give = add_halve(parts_a, parts_b, me["zl"])
     first_got = swap(first_give, "zl")
     first_mine = first_keep + first_got[:48].astype(F32)

time: 296 us -> 293 us (0.990)
  waiting for transfers between devices: 105 us -> 101 us
    unnamed x89 -> x85, local copies, waits for them, and re-layouts: 9.59 us -> 9.1 us
  transfers between devices with their start and end apart: 38 -> 38, of which waited for: 18 -> 17; matrix products, arithmetic and copies ran while one was open for 7% -> 8% of each run, Pallas kernels for 20% -> 20%
where the time goes in v1:
time: 293 us; the launch traced here: 289 us
  Pallas kernels  102 us (35%)
  waiting for transfers between devices  101 us (34%)
  starting transfers between devices  33.4 us (11%)
  other arithmetic  19.3 us (7%)
  local copies, waits for them, and re-layouts  19.1 us (7%)
  between operations  14.7 us (5%)
    ppermute x30, waiting for transfers between devices, shift(): return lax.ppermute(value, axis, [(i, (i - by) % n) for i in range(n)])  80.4 us
    pallas_call x1, Pallas kernels, scan_backward(): pl.pallas_call(scan_backward_kernel, grid_spec=pltpu.PrefetchScalarGridSp...  43.4 us
    ppermute x30, starting transfers between devices, shift(): return lax.ppermute(value, axis, [(i, (i - by) % n) for i in range(n)])  26.1 us
    pallas_call x1, Pallas kernels, scan_forward(): pl.pallas_call(scan_forward_kernel, grid=(blocks,), in_specs=[pl.BlockSpe...  24.1 us
    pallas_call x1, Pallas kernels, mix_second(): pl.pallas_call(lambda *refs: mix_second_kernel(channels, *refs), grid_spe...  18.9 us
    all_gather x1, waiting for transfers between devices, per_device(): lax.all_gather(pair_rows(main_rows, side_rows), ('y', 'x'), axis=0, tiled...  14 us
    unnamed x85, local copies, waits for them, and re-layouts  9.1 us
    pallas_call x2, Pallas kernels, place(): pl.pallas_call(place_kernel, grid_spec=pltpu.PrefetchScalarGridSpec(num_s...  8.28 us
  transfers between devices with their start and end apart: 38, of which 17 were waited for; matrix products, arithmetic and copies ran while one was open for 8% of the time, Pallas kernels for 20%

profile of v1, /device:TPU:24, one launch (start us, length us, event | category | flops | bytes accessed | tf_op | source)
XLA Modules:
  0.0 289.3 jit_solution(11508206072552933716)
XLA Ops:
  9.5 2.0 collective-permute-start.6
  11.5 3.6 %collective-permute-start.8 = (bf16[12,256]{1,0:T(8,128)(2,1)}, bf16[12,256]{1,0:T(8,128)(2,1)S(1)}, u32[]{:S(2)}, u32[]{:S(2)}) collective-permute-start(bf16[12,256]{1,0:T(8,128)(2,1)} %param.17), channel_id=1, source_target_pairs={{0,2},{1,3},{2,0},{3,1},{4,6},{5,7},{6,4},{7,5},{8,10},{9,11},{10,... | collective-permute-start | bytes 18440 | tf_op jit(solution)/shard_map/ppermute | solution.py:720
  16.5 4.0 %collective-permute-done.8 = bf16[12,256]{1,0:T(8,128)(2,1)S(1)} collective-permute-done((bf16[12,256]{1,0:T(8,128)(2,1)}, bf16[12,256]{1,0:T(8,128)(2,1)S(1)}, u32[]{:S(2)}, u32[]{:S(2)}) %collective-permute-start.8) | collective-permute-done | bytes 6176 | tf_op jit(solution)/shard_map/ppermute | solution.py:720
  20.9 3.9 %collective-permute-done.10.other_side = bf16[48,384]{1,0:T(8,128)(2,1)S(1)} collective-permute-done((bf16[48,384]{1,0:T(8,128)(2,1)S(1)}, bf16[48,384]{1,0:T(8,128)(2,1)S(1)}, u32[]{:S(2)}, u32[]{:S(2)}) %collective-permute-start.10) | collective-permute-done | bytes 36896 | tf_op jit(solution)/shard_map/ppermute | solution.py:702
  25.5 1.9 pair_rows.1
  29.5 18.4 %collective-permute-done.1.refs_2_ = bf16[256,1536]{1,0:T(8,128)(2,1)S(1)} collective-permute-done((bf16[256,1536]{1,0:T(8,128)(2,1)S(1)}, bf16[256,1536]{1,0:T(8,128)(2,1)S(1)}, u32[]{:S(2)}, u32[]{:S(2)}) %collective-permute-start.1) | collective-permute-done | bytes 786464 | tf_op jit(solution)/shard_map/ppermute | solution.py:702
  51.9 14.9 %collective-permute-done.4.refs_2_ = bf16[256,1536]{1,0:T(8,128)(2,1)} collective-permute-done((bf16[256,1536]{1,0:T(8,128)(2,1)S(1)}, bf16[256,1536]{1,0:T(8,128)(2,1)}, u32[]{:S(2)}, u32[]{:S(2)}) %collective-permute-start.4) | collective-permute-done | bytes 786464 | tf_op jit(solution)/shard_map/ppermute | solution.py:702
  72.1 4.1 %place_tokens.2.tok.refs_8_ = bf16[1024,1536]{1,0:T(8,128)(2,1)} custom-call(s32[1]{0:T(128)} %bitcast.me.refs_0_, bf16[256,1536]{1,0:T(8,128)(2,1)} %copy-done.1, bf16[256,1536]{1,0:T(8,128)(2,1)} %collective-permute-done.refs_1_, bf16[256,1536]{1,0:T(8,128)(2,1)} %copy-done.6, bf16[256,1536]{1,0:T(8,128)(2,1)} %copy-done.9), custom_call_target="tpu_custom_call" | custom-call | flops 2000000 | bytes 6000 | tf_op jit(solution)/shard_map/place_tokens/pallas_call | solution.py:685
  78.0 4.2 %place_tokens.3.rows.refs_9_ = bf16[1024,1536]{1,0:T(8,128)(2,1)} custom-call(s32[1]{0:T(128)} %bitcast.me.refs_0_, bf16[256,1536]{1,0:T(8,128)(2,1)} %refs_0_.1, bf16[256,1536]{1,0:T(8,128)(2,1)} %copy-done.7, bf16[256,1536]{1,0:T(8,128)(2,1)} %collective-permute-done.4.refs_2_, bf16[256,1536]{1,0:T(8,128)(2,1)} %copy-done.8), custom_call_target="tpu_custom_call" | custom-call | flops 2000000 | bytes 6000 | tf_op jit(solution)/shard_map/place_tokens/pallas_call | solution.py:685
  82.2 14.0 %all-gather.2.cloned.1.call-done.gate_w.out_a.out_b.weights_a.weights_b.weights_c.refs_5_.refs_6_.weights = bf16[1536,2688]{1,0:T(8,128)(2,1)} async-done(((bf16[96,2688]{1,0:T(8,128)(2,1)}), bf16[1536,2688]{1,0:T(8,128)(2,1)}) %all-gather.2.cloned.1.call-update) | async-done | bytes 8257552 | tf_op jit(solution)/shard_map/all_gather | solution.py:802
  96.2 24.1 %scan_forward.1 = (f32[1024,1152]{1,0:T(8,128)}, bf16[1024,768]{1,0:T(8,128)(2,1)}, bf16[8,128,768]{2,1,0:T(8,128)(2,1)}, bf16[1024,768]{1,0:T(8,128)(2,1)}, bf1...) custom-call(bf16[1024,1536]{1,0:T(8,128)(2,1)} %place_tokens.2.tok.refs_8_, bf16[1024,1536]{1,0:T(8,128)(2,1)} %place_tokens.3.rows.refs_9_, ...), custom_call_target="tpu_custom_call" | custom-call | flops 20000000 | bytes 60000 | tf_op jit(solution)/shard_map/scan_forward/pallas_call | solution.py:383
  122.6 3.2 %collective-permute-start.12 = (f32[8,1024]{1,0:T(8,128)S(1)}, f32[8,1024]{1,0:T(8,128)S(1)}, u32[]{:S(2)}, u32[]{:S(2)}) collective-permute-start(f32[8,1024]{1,0:T(8,128)S(1)} %add.179), channel_id=1, source_target_pairs={{0,2},{2,0},{1,3},{3,1},{4,6},{6,4},{5,7},{7,5},{8,10},{10,8},{9,1... | collective-permute-start | bytes 98312 | tf_op jit(solution)/shard_map/ppermute | solution.py:702
  125.7 2.3 collective-permute-done.12
  128.6 18.9 %mix_second.1 = (bf16[1024,768]{1,0:T(8,128)(2,1)}, bf16[1024,768]{1,0:T(8,128)(2,1)}, f32[8,768]{1,0:T(8,128)}, bf16[1536,1536]{1,0:T(8,128)(2,1)}, bf16[256,15...) custom-call(s32[1]{0:T(128)} %bitcast.me.refs_0_, ...), custom_call_target="tpu_custom_call" | custom-call | flops 11000000 | bytes 33000 | tf_op jit(solution)/shard_map/mix_second/pallas_call | solution.py:575
  149.1 2.9 collective-permute-done.14
  152.2 3.3 %collective-permute-start.15 = (bf16[256,1536]{1,0:T(8,128)(2,1)S(1)}, bf16[256,1536]{1,0:T(8,128)(2,1)S(1)}, u32[]{:S(2)}, u32[]{:S(2)}) collective-permute-start(bf16[256,1536]{1,0:T(8,128)(2,1)S(1)} %add_convert_fusion.1), channel_id=1, source_target_pairs={{0,2},{2,0},{1,3},{3,1},{4,6},{6,4},{5,7},{7,5},{8,10},{10,8},{9,1... | collective-permute-start | bytes 2359304 | tf_op jit(solution)/shard_map/ppermute | solution.py:702
  156.1 43.4 %scan_backward.1 = (bf16[256,1536]{1,0:T(8,128)(2,1)}, bf16[256,1536]{1,0:T(8,128)(2,1)}, bf16[256,1536]{1,0:T(8,128)(2,1)}, bf16[256,1536]{1,0:T(8,128)(2,1)}, ...) custom-call(s32[3]{0:T(128)} %pad_add_fusion.2.me, ...), custom_call_target="tpu_custom_call" | custom-call | flops 30000000 | bytes 90000 | tf_op jit(solution)/shard_map/scan_backward/pallas_call | solution.py:447
  199.6 2.5 collective-permute-done.16
  202.1 2.2 add_convert_fusion
  205.2 2.4 collective-permute-start.17
  210.5 8.0 %collective-permute-done.18.refs_3_ = bf16[4,96,512]{2,1,0:T(8,128)(2,1)S(1)} collective-permute-done((bf16[4,96,512]{2,1,0:T(8,128)(2,1)}, bf16[4,96,512]{2,1,0:T(8,128)(2,1)S(1)}, u32[]{:S(2)}, u32[]{:S(2)}) %collective-permute-start.18) | collective-permute-done | bytes 393248 | tf_op jit(solution)/shard_map/ppermute | solution.py:702
  220.9 4.9 %collective-permute-done.22.refs_7_ = bf16[416,640]{1,0:T(8,128)(2,1)S(1)} collective-permute-done((bf16[416,640]{1,0:T(8,128)(2,1)S(1)}, bf16[416,640]{1,0:T(8,128)(2,1)S(1)}, u32[]{:S(2)}, u32[]{:S(2)}) %collective-permute-start.22) | collective-permute-done | bytes 532512 | tf_op jit(solution)/shard_map/ppermute | solution.py:702
  225.8 2.0 collective-permute-done.21.refs_6_
  227.8 11.6 %collective-permute-done.20.refs_5_ = bf16[416,640]{1,0:T(8,128)(2,1)S(1)} collective-permute-done((bf16[416,640]{1,0:T(8,128)(2,1)S(1)}, bf16[416,640]{1,0:T(8,128)(2,1)S(1)}, u32[]{:S(2)}, u32[]{:S(2)}) %collective-permute-start.20) | collective-permute-done | bytes 532512 | tf_op jit(solution)/shard_map/ppermute | solution.py:702
  240.9 3.3 %add_split.1 = (bf16[96,512]{1,0:T(8,128)(2,1)}, bf16[96,512]{1,0:T(8,128)(2,1)}, bf16[96,512]{1,0:T(8,128)(2,1)}, bf16[96,512]{1,0:T(8,128)(2,1)}, bf16[128,640...) custom-call(s32[2]{0:T(128)} %pad_add_fusion.3.me, ...), custom_call_target="tpu_custom_call" | custom-call | tf_op jit(solution)/shard_map/add_split/pallas_call | solution.py:632
  244.4 3.2 %collective-permute-start.28 = (bf16[128,640]{1,0:T(8,128)(2,1)}, bf16[128,640]{1,0:T(8,128)(2,1)S(1)}, u32[]{:S(2)}, u32[]{:S(2)}) collective-permute-start(bf16[128,640]{1,0:T(8,128)(2,1)} %get-tuple-element.151), channel_id=1, source_target_pairs={{0,32},{32,64},{64,96},{96,0},{1,33},{33,65},{65,97},{97,1},{2,34}... | collective-permute-start | bytes 491528 | tf_op jit(solution)/shard_map/ppermute | solution.py:702
  248.4 3.9 %collective-permute-done.29.refs_7_ = bf16[128,640]{1,0:T(8,128)(2,1)S(1)} collective-permute-done((bf16[128,640]{1,0:T(8,128)(2,1)}, bf16[128,640]{1,0:T(8,128)(2,1)S(1)}, u32[]{:S(2)}, u32[]{:S(2)}) %collective-permute-start.29) | collective-permute-done | bytes 163872 | tf_op jit(solution)/shard_map/ppermute | solution.py:702
  254.0 1.7 fusion.8
  257.5 4.1 %fusion.7 = (bf16[256,1536]{1,0:T(8,128)(2,1)}, bf16[256,1536]{1,0:T(8,128)(2,1)}) fusion(bf16[256,1536]{1,0:T(8,128)(2,1)S(1)} %copy-done, bf16[256,1536]{1,0:T(8,128)(2,1)S(1)} %copy-done.3, bf16[256,1536]{1,0:T(8,128)(2,1)S(1)} %collective-permute-done.24, bf16[256,1536]{1,0:T(8,128)(2,1)} %collective-permute-done.23, bf16[256,1536]{1,0:T(8,128)(2,1)S(1)} %copy-done.4, ...), kind=kLoop, calls=%fused_computation.12 | loop fusion | flops 8650752 | bytes 7873536 | tf_op jit(solution)/shard_map/convert_element_type | solution.py:881
  261.6 2.2 add_halve.1
  266.0 3.7 %collective-permute-done.31 = bf16[80,1152]{1,0:T(8,128)(2,1)S(1)} collective-permute-done((bf16[80,1152]{1,0:T(8,128)(2,1)}, bf16[80,1152]{1,0:T(8,128)(2,1)S(1)}, u32[]{:S(2)}, u32[]{:S(2)}) %collective-permute-start.31) | collective-permute-done | bytes 184352 | tf_op jit(solution)/shard_map/ppermute | solution.py:702
  273.1 1.9 collective-permute-start.33
  (213 shorter events, 47.9 us)
Async XLA Ops:
  7.2 89.0 %all-gather.2.cloned.1.call-start = ((), (), s32[]{:S(2)}) async-start(), calls=%async_computation.1 | async-start | bytes 8773632 | tf_op jit(solution)/shard_map/all_gather | solution.py:802
  9.5 15.3 %collective-permute-start.6 = (bf16[48,2304]{1,0:T(8,128)(2,1)S(1)}, bf16[48,2304]{1,0:T(8,128)(2,1)S(1)}, u32[]{:S(2)}, u32[]{:S(2)}) collective-permute-start(bf16[48,2304]{1,0:T(8,128)(2,1)S(1)} %pad_maximum_fusion.1.main), channel_id=1, source_target_pairs={{0,4},{4,0},{1,5},{5,1},{2,6},{6,2},{3,7},{7,3},{8,12},{12,8},{9,1... | collective-permute-start | bytes 663560 | tf_op jit(solution)/shard_map/ppermute | solution.py:702
  11.5 9.0 %collective-permute-start.8 = (bf16[12,256]{1,0:T(8,128)(2,1)}, bf16[12,256]{1,0:T(8,128)(2,1)S(1)}, u32[]{:S(2)}, u32[]{:S(2)}) collective-permute-start(bf16[12,256]{1,0:T(8,128)(2,1)} %param.17), channel_id=1, source_target_pairs={{0,2},{1,3},{2,0},{3,1},{4,6},{5,7},{6,4},{7,5},{8,10},{9,11},{10,... | collective-permute-start | bytes 18440 | tf_op jit(solution)/shard_map/ppermute | solution.py:720
  15.1 5.5 %collective-permute-start.9 = (bf16[12,256]{1,0:T(8,128)(2,1)}, bf16[12,256]{1,0:T(8,128)(2,1)S(1)}, u32[]{:S(2)}, u32[]{:S(2)}) collective-permute-start(bf16[12,256]{1,0:T(8,128)(2,1)} %param.17), channel_id=1, source_target_pairs={{0,3},{1,2},{2,1},{3,0},{4,7},{5,6},{6,5},{7,4},{8,11},{9,10},{10,... | collective-permute-start | bytes 18440 | tf_op jit(solution)/shard_map/ppermute | solution.py:720
  27.5 228.4 %reduce-scatter.2.cloned.1.call-start = ((), (), s32[]{:S(2)}) async-start(), calls=%async_computation.2 | async-start | bytes 5013504 | tf_op jit(solution)/shard_map/reduce_scatter | solution.py:841
  28.1 19.8 %collective-permute-start.1 = (bf16[256,1536]{1,0:T(8,128)(2,1)S(1)}, bf16[256,1536]{1,0:T(8,128)(2,1)S(1)}, u32[]{:S(2)}, u32[]{:S(2)}) collective-permute-start(bf16[256,1536]{1,0:T(8,128)(2,1)S(1)} %fusion.2.refs_0_), channel_id=1, source_target_pairs={{0,2},{2,0},{1,3},{3,1},{4,6},{6,4},{5,7},{7,5},{8,10},{10,8},{9,1... | collective-permute-start | bytes 2359304 | tf_op jit(solution)/shard_map/ppermute | solution.py:702
  28.2 43.1 %collective-permute-start = (bf16[256,1536]{1,0:T(8,128)(2,1)S(1)}, bf16[256,1536]{1,0:T(8,128)(2,1)}, u32[]{:S(2)}, u32[]{:S(2)}) collective-permute-start(bf16[256,1536]{1,0:T(8,128)(2,1)S(1)} %fusion.2.refs_0_), channel_id=1, source_target_pairs={{0,1},{1,0},{2,3},{3,2},{4,5},{5,4},{6,7},{7,6},{8,9},{9,8},{10,11... | collective-permute-start | bytes 2359304 | tf_op jit(solution)/shard_map/ppermute | solution.py:702
  47.9 18.9 %collective-permute-start.4 = (bf16[256,1536]{1,0:T(8,128)(2,1)S(1)}, bf16[256,1536]{1,0:T(8,128)(2,1)}, u32[]{:S(2)}, u32[]{:S(2)}) collective-permute-start(bf16[256,1536]{1,0:T(8,128)(2,1)S(1)} %copy-done.2), channel_id=1, source_target_pairs={{0,2},{2,0},{1,3},{3,1},{4,6},{6,4},{5,7},{7,5},{8,10},{10,8},{9,1... | collective-permute-start | bytes 2359304 | tf_op jit(solution)/shard_map/ppermute | solution.py:702
  51.4 24.9 %collective-permute-start.3 = (bf16[256,1536]{1,0:T(8,128)(2,1)S(1)}, bf16[256,1536]{1,0:T(8,128)(2,1)S(1)}, u32[]{:S(2)}, u32[]{:S(2)}) collective-permute-start(bf16[256,1536]{1,0:T(8,128)(2,1)S(1)} %copy-done.2), channel_id=1, source_target_pairs={{0,1},{1,0},{2,3},{3,2},{4,5},{5,4},{6,7},{7,6},{8,9},{9,8},{10,11... | collective-permute-start | bytes 2359304 | tf_op jit(solution)/shard_map/ppermute | solution.py:702
  51.4 19.9 %collective-permute-start.2 = (bf16[256,1536]{1,0:T(8,128)(2,1)}, bf16[256,1536]{1,0:T(8,128)(2,1)S(1)}, u32[]{:S(2)}, u32[]{:S(2)}) collective-permute-start(bf16[256,1536]{1,0:T(8,128)(2,1)} %copy-done.6), channel_id=1, source_target_pairs={{0,1},{1,0},{2,3},{3,2},{4,5},{5,4},{6,7},{7,6},{8,9},{9,8},{10,11... | collective-permute-start | bytes 2359304 | tf_op jit(solution)/shard_map/ppermute | solution.py:702
  66.8 9.4 %collective-permute-start.5 = (bf16[256,1536]{1,0:T(8,128)(2,1)}, bf16[256,1536]{1,0:T(8,128)(2,1)S(1)}, u32[]{:S(2)}, u32[]{:S(2)}) collective-permute-start(bf16[256,1536]{1,0:T(8,128)(2,1)} %collective-permute-done.4.refs_2_), channel_id=1, source_target_pairs={{0,1},{1,0},{2,3},{3,2},{4,5},{5,4},{6,7},{7,6},{8,9},{9,8},{10,11... | collective-permute-start | bytes 2359304 | tf_op jit(solution)/shard_map/ppermute | solution.py:702
  122.6 5.4 %collective-permute-start.12 = (f32[8,1024]{1,0:T(8,128)S(1)}, f32[8,1024]{1,0:T(8,128)S(1)}, u32[]{:S(2)}, u32[]{:S(2)}) collective-permute-start(f32[8,1024]{1,0:T(8,128)S(1)} %add.179), channel_id=1, source_target_pairs={{0,2},{2,0},{1,3},{3,1},{4,6},{6,4},{5,7},{7,5},{8,10},{10,8},{9,1... | collective-permute-start | bytes 98312 | tf_op jit(solution)/shard_map/ppermute | solution.py:702
  148.6 50.9 %collective-permute-start.13 = (bf16[256,1536]{1,0:T(8,128)(2,1)}, bf16[256,1536]{1,0:T(8,128)(2,1)S(1)}, u32[]{:S(2)}, u32[]{:S(2)}) collective-permute-start(bf16[256,1536]{1,0:T(8,128)(2,1)} %get-tuple-element.103), channel_id=1, source_target_pairs={{0,1},{1,0},{2,3},{3,2},{4,5},{5,4},{6,7},{7,6},{8,9},{9,8},{10,11... | collective-permute-start | bytes 2359304 | tf_op jit(solution)/shard_map/ppermute | solution.py:702
  152.2 47.3 %collective-permute-start.15 = (bf16[256,1536]{1,0:T(8,128)(2,1)S(1)}, bf16[256,1536]{1,0:T(8,128)(2,1)S(1)}, u32[]{:S(2)}, u32[]{:S(2)}) collective-permute-start(bf16[256,1536]{1,0:T(8,128)(2,1)S(1)} %add_convert_fusion.1), channel_id=1, source_target_pairs={{0,2},{2,0},{1,3},{3,1},{4,6},{6,4},{5,7},{7,5},{8,10},{10,8},{9,1... | collective-permute-start | bytes 2359304 | tf_op jit(solution)/shard_map/ppermute | solution.py:702
  204.3 14.1 %collective-permute-start.18 = (bf16[4,96,512]{2,1,0:T(8,128)(2,1)}, bf16[4,96,512]{2,1,0:T(8,128)(2,1)S(1)}, u32[]{:S(2)}, u32[]{:S(2)}) collective-permute-start(bf16[4,96,512]{2,1,0:T(8,128)(2,1)} %get-tuple-element.130), channel_id=1, source_target_pairs={{0,96},{32,0},{64,32},{96,64},{1,97},{33,1},{65,33},{97,65},{2,98}... | collective-permute-start | bytes 1179656 | tf_op jit(solution)/shard_map/ppermute | solution.py:702
  205.2 13.3 %collective-permute-start.17 = (bf16[4,96,512]{2,1,0:T(8,128)(2,1)}, bf16[4,96,512]{2,1,0:T(8,128)(2,1)S(1)}, u32[]{:S(2)}, u32[]{:S(2)}) collective-permute-start(bf16[4,96,512]{2,1,0:T(8,128)(2,1)} %get-tuple-element.126), channel_id=1, source_target_pairs={{0,32},{32,64},{64,96},{96,0},{1,33},{33,65},{65,97},{97,1},{2,34}... | collective-permute-start | bytes 1179656 | tf_op jit(solution)/shard_map/ppermute | solution.py:702
  207.6 18.2 %collective-permute-start.22 = (bf16[416,640]{1,0:T(8,128)(2,1)S(1)}, bf16[416,640]{1,0:T(8,128)(2,1)S(1)}, u32[]{:S(2)}, u32[]{:S(2)}) collective-permute-start(bf16[416,640]{1,0:T(8,128)(2,1)S(1)} %copy-done.36), channel_id=1, source_target_pairs={{0,24},{8,0},{16,8},{24,16},{1,25},{9,1},{17,9},{25,17},{2,26},{10... | collective-permute-start | bytes 1597448 | tf_op jit(solution)/shard_map/ppermute | solution.py:702
  208.4 19.3 %collective-permute-start.21 = (bf16[416,640]{1,0:T(8,128)(2,1)S(1)}, bf16[416,640]{1,0:T(8,128)(2,1)S(1)}, u32[]{:S(2)}, u32[]{:S(2)}) collective-permute-start(bf16[416,640]{1,0:T(8,128)(2,1)S(1)} %copy-done.35), channel_id=1, source_target_pairs={{0,16},{8,24},{16,0},{24,8},{1,17},{9,25},{17,1},{25,9},{2,18},{10... | collective-permute-start | bytes 1597448 | tf_op jit(solution)/shard_map/ppermute | solution.py:702
  209.9 29.5 %collective-permute-start.20 = (bf16[416,640]{1,0:T(8,128)(2,1)S(1)}, bf16[416,640]{1,0:T(8,128)(2,1)S(1)}, u32[]{:S(2)}, u32[]{:S(2)}) collective-permute-start(bf16[416,640]{1,0:T(8,128)(2,1)S(1)} %copy-done.34), channel_id=1, source_target_pairs={{0,8},{8,16},{16,24},{24,0},{1,9},{9,17},{17,25},{25,1},{2,10},{10... | collective-permute-start | bytes 1597448 | tf_op jit(solution)/shard_map/ppermute | solution.py:702
  218.5 20.9 %collective-permute-start.19 = (bf16[4,96,512]{2,1,0:T(8,128)(2,1)S(1)}, bf16[4,96,512]{2,1,0:T(8,128)(2,1)S(1)}, u32[]{:S(2)}, u32[]{:S(2)}) collective-permute-start(bf16[4,96,512]{2,1,0:T(8,128)(2,1)S(1)} %copy-done.37), channel_id=1, source_target_pairs={{0,64},{32,96},{64,0},{96,32},{1,65},{33,97},{65,1},{97,33},{2,66}... | collective-permute-start | bytes 1179656 | tf_op jit(solution)/shard_map/ppermute | solution.py:702
  220.5 33.5 %collective-permute-start.24 = (bf16[256,1536]{1,0:T(8,128)(2,1)}, bf16[256,1536]{1,0:T(8,128)(2,1)S(1)}, u32[]{:S(2)}, u32[]{:S(2)}) collective-permute-start(bf16[256,1536]{1,0:T(8,128)(2,1)} %add_convert_fusion), channel_id=1, source_target_pairs={{0,2},{2,0},{1,3},{3,1},{4,6},{6,4},{5,7},{7,5},{8,10},{10,8},{9,1... | collective-permute-start | bytes 2359304 | tf_op jit(solution)/shard_map/ppermute | solution.py:702
  244.2 9.8 %collective-permute-start.23 = (bf16[256,1536]{1,0:T(8,128)(2,1)}, bf16[256,1536]{1,0:T(8,128)(2,1)}, u32[]{:S(2)}, u32[]{:S(2)}) collective-permute-start(bf16[256,1536]{1,0:T(8,128)(2,1)} %get-tuple-element.144), channel_id=1, source_target_pairs={{0,1},{1,0},{2,3},{3,2},{4,5},{5,4},{6,7},{7,6},{8,9},{9,8},{10,11... | collective-permute-start | bytes 2359304 | tf_op jit(solution)/shard_map/ppermute | solution.py:702
  244.3 8.0 %collective-permute-start.29 = (bf16[128,640]{1,0:T(8,128)(2,1)}, bf16[128,640]{1,0:T(8,128)(2,1)S(1)}, u32[]{:S(2)}, u32[]{:S(2)}) collective-permute-start(bf16[128,640]{1,0:T(8,128)(2,1)} %get-tuple-element.154), channel_id=1, source_target_pairs={{0,96},{32,0},{64,32},{96,64},{1,97},{33,1},{65,33},{97,65},{2,98}... | collective-permute-start | bytes 491528 | tf_op jit(solution)/shard_map/ppermute | solution.py:702
  244.4 9.4 %collective-permute-start.28 = (bf16[128,640]{1,0:T(8,128)(2,1)}, bf16[128,640]{1,0:T(8,128)(2,1)S(1)}, u32[]{:S(2)}, u32[]{:S(2)}) collective-permute-start(bf16[128,640]{1,0:T(8,128)(2,1)} %get-tuple-element.151), channel_id=1, source_target_pairs={{0,32},{32,64},{64,96},{96,0},{1,33},{33,65},{65,97},{97,1},{2,34}... | collective-permute-start | bytes 491528 | tf_op jit(solution)/shard_map/ppermute | solution.py:702
  247.6 14.0 %collective-permute-start.27 = (bf16[96,512]{1,0:T(8,128)(2,1)}, bf16[96,512]{1,0:T(8,128)(2,1)}, u32[]{:S(2)}, u32[]{:S(2)}) collective-permute-start(bf16[96,512]{1,0:T(8,128)(2,1)} %get-tuple-element.143), channel_id=1, source_target_pairs={{0,24},{8,0},{16,8},{24,16},{1,25},{9,1},{17,9},{25,17},{2,26},{10... | collective-permute-start | bytes 294920 | tf_op jit(solution)/shard_map/ppermute | solution.py:702
  252.3 9.3 %collective-permute-start.26 = (bf16[96,512]{1,0:T(8,128)(2,1)}, bf16[96,512]{1,0:T(8,128)(2,1)}, u32[]{:S(2)}, u32[]{:S(2)}) collective-permute-start(bf16[96,512]{1,0:T(8,128)(2,1)} %get-tuple-element.142), channel_id=1, source_target_pairs={{0,16},{8,24},{16,0},{24,8},{1,17},{9,25},{17,1},{25,9},{2,18},{10... | collective-permute-start | bytes 294920 | tf_op jit(solution)/shard_map/ppermute | solution.py:702
  253.8 7.9 %collective-permute-start.25 = (bf16[96,512]{1,0:T(8,128)(2,1)}, bf16[96,512]{1,0:T(8,128)(2,1)}, u32[]{:S(2)}, u32[]{:S(2)}) collective-permute-start(bf16[96,512]{1,0:T(8,128)(2,1)} %get-tuple-element.141), channel_id=1, source_target_pairs={{0,8},{8,16},{16,24},{24,0},{1,9},{9,17},{17,25},{25,1},{2,10},{10... | collective-permute-start | bytes 294920 | tf_op jit(solution)/shard_map/ppermute | solution.py:702
  254.0 7.6 %collective-permute-start.30 = (bf16[128,640]{1,0:T(8,128)(2,1)}, bf16[128,640]{1,0:T(8,128)(2,1)}, u32[]{:S(2)}, u32[]{:S(2)}) collective-permute-start(bf16[128,640]{1,0:T(8,128)(2,1)} %get-tuple-element.155), channel_id=1, source_target_pairs={{0,64},{32,96},{64,0},{96,32},{1,65},{33,97},{65,1},{97,33},{2,66}... | collective-permute-start | bytes 491528 | tf_op jit(solution)/shard_map/ppermute | solution.py:702
  256.8 8.5 %collective-permute-start.35 = (bf16[48,1536]{1,0:T(8,128)(2,1)S(1)}, bf16[48,1536]{1,0:T(8,128)(2,1)S(1)}, u32[]{:S(2)}, u32[]{:S(2)}) collective-permute-start(bf16[48,1536]{1,0:T(8,128)(2,1)S(1)} %dynamic-slice_bitcast_fusion), channel_id=1, source_target_pairs={{0,4},{4,0},{1,5},{5,1},{2,6},{6,2},{3,7},{7,3},{8,12},{12,8},{9,1... | collective-permute-start | bytes 442376 | tf_op jit(solution)/shard_map/ppermute | solution.py:702
  263.9 5.8 %collective-permute-start.31 = (bf16[80,1152]{1,0:T(8,128)(2,1)}, bf16[80,1152]{1,0:T(8,128)(2,1)S(1)}, u32[]{:S(2)}, u32[]{:S(2)}) collective-permute-start(bf16[80,1152]{1,0:T(8,128)(2,1)} %get-tuple-element.159), channel_id=1, source_target_pairs={{0,4},{4,0},{1,5},{5,1},{2,6},{6,2},{3,7},{7,3},{8,12},{12,8},{9,1... | collective-permute-start | bytes 552968 | tf_op jit(solution)/shard_map/ppermute | solution.py:702
  273.1 6.0 %collective-permute-start.33 = (f32[28,512]{1,0:T(8,128)S(1)}, f32[28,512]{1,0:T(8,128)S(1)}, u32[]{:S(2)}, u32[]{:S(2)}) collective-permute-start(f32[28,512]{1,0:T(8,128)S(1)} %get-tuple-element.231), channel_id=1, source_target_pairs={{0,2},{1,3},{2,0},{3,1},{4,6},{5,7},{6,4},{7,5},{8,10},{9,11},{10,... | collective-permute-start | bytes 172040 | tf_op jit(solution)/shard_map/ppermute | solution.py:720
  275.0 5.6 %collective-permute-start.34 = (f32[28,512]{1,0:T(8,128)S(1)}, f32[28,512]{1,0:T(8,128)S(1)}, u32[]{:S(2)}, u32[]{:S(2)}) collective-permute-start(f32[28,512]{1,0:T(8,128)S(1)} %get-tuple-element.229), channel_id=1, source_target_pairs={{0,3},{1,2},{2,1},{3,0},{4,7},{5,6},{6,5},{7,4},{8,11},{9,10},{10,... | collective-permute-start | bytes 172040 | tf_op jit(solution)/shard_map/ppermute | solution.py:720
  (45 other events, 549.4 us)
Sparse Core Ops, SparseCore 0:
  27.5 68.6 all-gather.1
  147.7 90.5 reduce-scatter.1

commit v2 on v1

--- a/solution.py
+++ b/solution.py
@@ -347,7 +347,6 @@
         sums_low = small_rows(jnp.concatenate([packed[:, :512], packed[:, 512:]], 0))
         for k in range(4):
             outs_b[k][4 * deep :, :512] = sums_low
-            outs_b[k][4 * deep :, 512:] = jnp.zeros((32, outs_b[k].shape[1] - 512), BF16)
 
 
 def scan_marks(segments):
@@ -435,7 +434,7 @@
     wide = cols - 128
     n = BACKWARD_BLOCK
     blocks = length // n
-    cut = 512
+    cut = 640
     shape_a, shape_b = (4, model // 16, cut), (model // 4 + 32, cols - cut)
 
     def rev(i):
@@ -623,7 +622,6 @@
         place = pl.ds(pl.multiple_of(((me[1] + d) % 4) * deep, 16), deep)
         outs_b[d][:deep, :] = four_sum(*[part[place, :] for part in parts_b]).astype(BF16)
         outs_b[d][deep:, :512] = sums
-        outs_b[d][deep:, 512:] = jnp.zeros((32, outs_b[d].shape[1] - 512), BF16)
 
 
 def add_split(parts_a, parts_b, me):
@@ -864,8 +862,8 @@
     far_got = swap(row_blocks[0], "c")
     row_far = (row_blocks[1].astype(F32) + far_got.astype(F32)).astype(BF16)
     row_far_got = swap(row_far, "zh")
-    parts_b = sends([after(block, row_far) for block in sent[8:]], "x")
-    parts_a = sends([after(block, row_far) for block in sent[4:8]], "y", in_turn=True)
+    parts_b = sends([after(block, row_far) for block in sent[8:]], "x", in_turn=True)
+    parts_a = sends([after(block, row_far) for block in sent[4:8]], "y")
     half_a, half_b = add_split(parts_a, parts_b, jnp.concatenate([me["x"], me["y"]]))
     near_got = swap(after(row_blocks[2], *half_a), "c")
 

time: 293 us -> 292 us (level)
  waiting for transfers between devices: 101 us -> 96.7 us
    ppermute x30, waiting for transfers between devices: 80.4 us -> 76.8 us  [shift(): return lax.ppermute(value, axis, [(i, (i - by) % n) for i in range(n)])]
    unnamed x85 -> x89, local copies, waits for them, and re-layouts: 9.1 us -> 9.7 us
  transfers between devices with their start and end apart: 38 -> 38, of which waited for: 17 -> 18; matrix products, arithmetic and copies ran while one was open for 8% -> 8% of each run, Pallas kernels for 20% -> 20%
where the time goes in v2:
time: 292 us; the launch traced here: 288 us
  Pallas kernels  102 us (35%)
  waiting for transfers between devices  96.7 us (33%)
  starting transfers between devices  35.1 us (12%)
  other arithmetic  19.9 us (7%)
  local copies, waits for them, and re-layouts  19.8 us (7%)
  between operations  14.7 us (5%)
    ppermute x30, waiting for transfers between devices, shift(): return lax.ppermute(value, axis, [(i, (i - by) % n) for i in range(n)])  76.8 us
    pallas_call x1, Pallas kernels, scan_backward(): pl.pallas_call(scan_backward_kernel, grid_spec=pltpu.PrefetchScalarGridSp...  43.2 us
    ppermute x30, starting transfers between devices, shift(): return lax.ppermute(value, axis, [(i, (i - by) % n) for i in range(n)])  27.9 us
    pallas_call x1, Pallas kernels, scan_forward(): pl.pallas_call(scan_forward_kernel, grid=(blocks,), in_specs=[pl.BlockSpe...  24.1 us
    pallas_call x1, Pallas kernels, mix_second(): pl.pallas_call(lambda *refs: mix_second_kernel(channels, *refs), grid_spe...  18.9 us
    all_gather x1, waiting for transfers between devices, per_device(): lax.all_gather(pair_rows(main_rows, side_rows), ('y', 'x'), axis=0, tiled...  13.6 us
    unnamed x89, local copies, waits for them, and re-layouts  9.7 us
    pallas_call x2, Pallas kernels, place(): pl.pallas_call(place_kernel, grid_spec=pltpu.PrefetchScalarGridSpec(num_s...  8.23 us
  transfers between devices with their start and end apart: 38, of which 18 were waited for; matrix products, arithmetic and copies ran while one was open for 8% of the time, Pallas kernels for 20%

profile of v2, /device:TPU:24, one launch (start us, length us, event | category | flops | bytes accessed | tf_op | source)
XLA Modules:
  0.0 287.9 jit_solution(6970319520227791895)
XLA Ops:
  9.5 2.0 collective-permute-start.6
  11.5 3.6 %collective-permute-start.8 = (bf16[12,256]{1,0:T(8,128)(2,1)}, bf16[12,256]{1,0:T(8,128)(2,1)S(1)}, u32[]{:S(2)}, u32[]{:S(2)}) collective-permute-start(bf16[12,256]{1,0:T(8,128)(2,1)} %param.17), channel_id=1, source_target_pairs={{0,2},{1,3},{2,0},{3,1},{4,6},{5,7},{6,4},{7,5},{8,10},{9,11},{10,... | collective-permute-start | bytes 18440 | tf_op jit(solution)/shard_map/ppermute | solution.py:718
  16.5 4.0 %collective-permute-done.8 = bf16[12,256]{1,0:T(8,128)(2,1)S(1)} collective-permute-done((bf16[12,256]{1,0:T(8,128)(2,1)}, bf16[12,256]{1,0:T(8,128)(2,1)S(1)}, u32[]{:S(2)}, u32[]{:S(2)}) %collective-permute-start.8) | collective-permute-done | bytes 6176 | tf_op jit(solution)/shard_map/ppermute | solution.py:718
  20.9 3.9 %collective-permute-done.10.other_side = bf16[48,384]{1,0:T(8,128)(2,1)S(1)} collective-permute-done((bf16[48,384]{1,0:T(8,128)(2,1)S(1)}, bf16[48,384]{1,0:T(8,128)(2,1)S(1)}, u32[]{:S(2)}, u32[]{:S(2)}) %collective-permute-start.10) | collective-permute-done | bytes 36896 | tf_op jit(solution)/shard_map/ppermute | solution.py:700
  25.5 1.9 pair_rows.1
  30.1 18.4 %collective-permute-done.1.refs_2_ = bf16[256,1536]{1,0:T(8,128)(2,1)S(1)} collective-permute-done((bf16[256,1536]{1,0:T(8,128)(2,1)S(1)}, bf16[256,1536]{1,0:T(8,128)(2,1)S(1)}, u32[]{:S(2)}, u32[]{:S(2)}) %collective-permute-start.1) | collective-permute-done | bytes 786464 | tf_op jit(solution)/shard_map/ppermute | solution.py:700
  52.4 15.0 %collective-permute-done.4.refs_2_ = bf16[256,1536]{1,0:T(8,128)(2,1)} collective-permute-done((bf16[256,1536]{1,0:T(8,128)(2,1)S(1)}, bf16[256,1536]{1,0:T(8,128)(2,1)}, u32[]{:S(2)}, u32[]{:S(2)}) %collective-permute-start.4) | collective-permute-done | bytes 786464 | tf_op jit(solution)/shard_map/ppermute | solution.py:700
  72.7 4.1 %place_tokens.2.tok.refs_8_ = bf16[1024,1536]{1,0:T(8,128)(2,1)} custom-call(s32[1]{0:T(128)} %bitcast.me.refs_0_, bf16[256,1536]{1,0:T(8,128)(2,1)} %copy-done.1, bf16[256,1536]{1,0:T(8,128)(2,1)} %collective-permute-done.refs_1_, bf16[256,1536]{1,0:T(8,128)(2,1)} %copy-done.6, bf16[256,1536]{1,0:T(8,128)(2,1)} %copy-done.9), custom_call_target="tpu_custom_call" | custom-call | flops 2000000 | bytes 6000 | tf_op jit(solution)/shard_map/place_tokens/pallas_call | solution.py:683
  78.5 4.1 %place_tokens.3.rows.refs_9_ = bf16[1024,1536]{1,0:T(8,128)(2,1)} custom-call(s32[1]{0:T(128)} %bitcast.me.refs_0_, bf16[256,1536]{1,0:T(8,128)(2,1)} %refs_0_.1, bf16[256,1536]{1,0:T(8,128)(2,1)} %copy-done.7, bf16[256,1536]{1,0:T(8,128)(2,1)} %collective-permute-done.4.refs_2_, bf16[256,1536]{1,0:T(8,128)(2,1)} %copy-done.8), custom_call_target="tpu_custom_call" | custom-call | flops 2000000 | bytes 6000 | tf_op jit(solution)/shard_map/place_tokens/pallas_call | solution.py:683
  82.7 13.6 %all-gather.2.cloned.1.call-done.gate_w.out_a.out_b.weights_a.weights_b.weights_c.refs_5_.refs_6_.weights = bf16[1536,2688]{1,0:T(8,128)(2,1)} async-done(((bf16[96,2688]{1,0:T(8,128)(2,1)}), bf16[1536,2688]{1,0:T(8,128)(2,1)}) %all-gather.2.cloned.1.call-update) | async-done | bytes 8257552 | tf_op jit(solution)/shard_map/all_gather | solution.py:800
  96.2 24.1 %scan_forward.1 = (f32[1024,1152]{1,0:T(8,128)}, bf16[1024,768]{1,0:T(8,128)(2,1)}, bf16[8,128,768]{2,1,0:T(8,128)(2,1)}, bf16[1024,768]{1,0:T(8,128)(2,1)}, bf1...) custom-call(bf16[1024,1536]{1,0:T(8,128)(2,1)} %place_tokens.2.tok.refs_8_, bf16[1024,1536]{1,0:T(8,128)(2,1)} %place_tokens.3.rows.refs_9_, ...), custom_call_target="tpu_custom_call" | custom-call | flops 20000000 | bytes 60000 | tf_op jit(solution)/shard_map/scan_forward/pallas_call | solution.py:382
  122.6 3.2 %collective-permute-start.12 = (f32[8,1024]{1,0:T(8,128)S(1)}, f32[8,1024]{1,0:T(8,128)S(1)}, u32[]{:S(2)}, u32[]{:S(2)}) collective-permute-start(f32[8,1024]{1,0:T(8,128)S(1)} %add.179), channel_id=1, source_target_pairs={{0,2},{2,0},{1,3},{3,1},{4,6},{6,4},{5,7},{7,5},{8,10},{10,8},{9,1... | collective-permute-start | bytes 98312 | tf_op jit(solution)/shard_map/ppermute | solution.py:700
  125.8 2.3 collective-permute-done.12
  128.6 18.9 %mix_second.1 = (bf16[1024,768]{1,0:T(8,128)(2,1)}, bf16[1024,768]{1,0:T(8,128)(2,1)}, f32[8,768]{1,0:T(8,128)}, bf16[1536,1536]{1,0:T(8,128)(2,1)}, bf16[256,15...) custom-call(s32[1]{0:T(128)} %bitcast.me.refs_0_, ...), custom_call_target="tpu_custom_call" | custom-call | flops 11000000 | bytes 33000 | tf_op jit(solution)/shard_map/mix_second/pallas_call | solution.py:574
  149.2 2.9 collective-permute-done.14
  152.2 3.3 %collective-permute-start.15 = (bf16[256,1536]{1,0:T(8,128)(2,1)S(1)}, bf16[256,1536]{1,0:T(8,128)(2,1)S(1)}, u32[]{:S(2)}, u32[]{:S(2)}) collective-permute-start(bf16[256,1536]{1,0:T(8,128)(2,1)S(1)} %add_convert_fusion.1), channel_id=1, source_target_pairs={{0,2},{2,0},{1,3},{3,1},{4,6},{6,4},{5,7},{7,5},{8,10},{10,8},{9,1... | collective-permute-start | bytes 2359304 | tf_op jit(solution)/shard_map/ppermute | solution.py:700
  156.1 43.2 %scan_backward.1 = (bf16[256,1536]{1,0:T(8,128)(2,1)}, bf16[256,1536]{1,0:T(8,128)(2,1)}, bf16[256,1536]{1,0:T(8,128)(2,1)}, bf16[256,1536]{1,0:T(8,128)(2,1)}, ...) custom-call(s32[3]{0:T(128)} %pad_add_fusion.2.me, ...), custom_call_target="tpu_custom_call" | custom-call | flops 30000000 | bytes 90000 | tf_op jit(solution)/shard_map/scan_backward/pallas_call | solution.py:446
  199.5 2.5 collective-permute-done.16
  202.0 2.2 add_convert_fusion
  207.1 1.9 collective-permute-start.18
  210.3 7.7 %collective-permute-done.21.refs_7_ = bf16[416,512]{1,0:T(8,128)(2,1)S(1)} collective-permute-done((bf16[416,512]{1,0:T(8,128)(2,1)}, bf16[416,512]{1,0:T(8,128)(2,1)S(1)}, u32[]{:S(2)}, u32[]{:S(2)}) %collective-permute-start.21) | collective-permute-done | bytes 426016 | tf_op jit(solution)/shard_map/ppermute | solution.py:700
  218.0 2.7 collective-permute-done.20.refs_5_
  223.0 12.2 %collective-permute-done.18.refs_2_ = bf16[4,96,640]{2,1,0:T(8,128)(2,1)S(1)} collective-permute-done((bf16[4,96,640]{2,1,0:T(8,128)(2,1)S(1)}, bf16[4,96,640]{2,1,0:T(8,128)(2,1)S(1)}, u32[]{:S(2)}, u32[]{:S(2)}) %collective-permute-start.18) | collective-permute-done | bytes 491552 | tf_op jit(solution)/shard_map/ppermute | solution.py:700
  237.6 3.2 %add_split.1 = (bf16[96,640]{1,0:T(8,128)(2,1)}, bf16[96,640]{1,0:T(8,128)(2,1)}, bf16[96,640]{1,0:T(8,128)(2,1)}, bf16[96,640]{1,0:T(8,128)(2,1)}, bf16[128,512...) custom-call(s32[2]{0:T(128)} %pad_add_fusion.3.me, ...), custom_call_target="tpu_custom_call" | custom-call | tf_op jit(solution)/shard_map/add_split/pallas_call | solution.py:630
  241.7 2.5 collective-permute-start.28
  244.2 2.3 collective-permute-start.27
  246.4 1.8 collective-permute-done.29.refs_7_
  252.1 1.7 fusion.8
  255.5 4.1 %fusion.7 = (bf16[256,1536]{1,0:T(8,128)(2,1)}, bf16[256,1536]{1,0:T(8,128)(2,1)}) fusion(bf16[256,1536]{1,0:T(8,128)(2,1)S(1)} %copy-done, bf16[256,1536]{1,0:T(8,128)(2,1)S(1)} %copy-done.3, bf16[256,1536]{1,0:T(8,128)(2,1)S(1)} %collective-permute-done.24, bf16[256,1536]{1,0:T(8,128)(2,1)} %collective-permute-done.23, bf16[256,1536]{1,0:T(8,128)(2,1)S(1)} %copy-done.4, ...), kind=kLoop, calls=%fused_computation.12 | loop fusion | flops 8650752 | bytes 7873536 | tf_op jit(solution)/shard_map/convert_element_type | solution.py:879
  260.2 2.2 add_halve.1
  264.6 3.6 %collective-permute-done.31 = bf16[80,1152]{1,0:T(8,128)(2,1)S(1)} collective-permute-done((bf16[80,1152]{1,0:T(8,128)(2,1)}, bf16[80,1152]{1,0:T(8,128)(2,1)S(1)}, u32[]{:S(2)}, u32[]{:S(2)}) %collective-permute-start.31) | collective-permute-done | bytes 184352 | tf_op jit(solution)/shard_map/ppermute | solution.py:700
  271.7 1.9 collective-permute-start.33
  (217 shorter events, 52.4 us)
Async XLA Ops:
  7.2 89.0 %all-gather.2.cloned.1.call-start = ((), (), s32[]{:S(2)}) async-start(), calls=%async_computation.1 | async-start | bytes 8773632 | tf_op jit(solution)/shard_map/all_gather | solution.py:800
  9.5 15.3 %collective-permute-start.6 = (bf16[48,2304]{1,0:T(8,128)(2,1)S(1)}, bf16[48,2304]{1,0:T(8,128)(2,1)S(1)}, u32[]{:S(2)}, u32[]{:S(2)}) collective-permute-start(bf16[48,2304]{1,0:T(8,128)(2,1)S(1)} %pad_maximum_fusion.1.main), channel_id=1, source_target_pairs={{0,4},{4,0},{1,5},{5,1},{2,6},{6,2},{3,7},{7,3},{8,12},{12,8},{9,1... | collective-permute-start | bytes 663560 | tf_op jit(solution)/shard_map/ppermute | solution.py:700
  11.5 9.0 %collective-permute-start.8 = (bf16[12,256]{1,0:T(8,128)(2,1)}, bf16[12,256]{1,0:T(8,128)(2,1)S(1)}, u32[]{:S(2)}, u32[]{:S(2)}) collective-permute-start(bf16[12,256]{1,0:T(8,128)(2,1)} %param.17), channel_id=1, source_target_pairs={{0,2},{1,3},{2,0},{3,1},{4,6},{5,7},{6,4},{7,5},{8,10},{9,11},{10,... | collective-permute-start | bytes 18440 | tf_op jit(solution)/shard_map/ppermute | solution.py:718
  15.1 5.5 %collective-permute-start.9 = (bf16[12,256]{1,0:T(8,128)(2,1)}, bf16[12,256]{1,0:T(8,128)(2,1)S(1)}, u32[]{:S(2)}, u32[]{:S(2)}) collective-permute-start(bf16[12,256]{1,0:T(8,128)(2,1)} %param.17), channel_id=1, source_target_pairs={{0,3},{1,2},{2,1},{3,0},{4,7},{5,6},{6,5},{7,4},{8,11},{9,10},{10,... | collective-permute-start | bytes 18440 | tf_op jit(solution)/shard_map/ppermute | solution.py:718
  27.5 226.3 %reduce-scatter.2.cloned.1.call-start = ((), (), s32[]{:S(2)}) async-start(), calls=%async_computation.2 | async-start | bytes 5013504 | tf_op jit(solution)/shard_map/reduce_scatter | solution.py:839
  28.6 19.8 %collective-permute-start.1 = (bf16[256,1536]{1,0:T(8,128)(2,1)S(1)}, bf16[256,1536]{1,0:T(8,128)(2,1)S(1)}, u32[]{:S(2)}, u32[]{:S(2)}) collective-permute-start(bf16[256,1536]{1,0:T(8,128)(2,1)S(1)} %fusion.2.refs_0_), channel_id=1, source_target_pairs={{0,2},{2,0},{1,3},{3,1},{4,6},{6,4},{5,7},{7,5},{8,10},{10,8},{9,1... | collective-permute-start | bytes 2359304 | tf_op jit(solution)/shard_map/ppermute | solution.py:700
  28.7 43.1 %collective-permute-start = (bf16[256,1536]{1,0:T(8,128)(2,1)S(1)}, bf16[256,1536]{1,0:T(8,128)(2,1)}, u32[]{:S(2)}, u32[]{:S(2)}) collective-permute-start(bf16[256,1536]{1,0:T(8,128)(2,1)S(1)} %fusion.2.refs_0_), channel_id=1, source_target_pairs={{0,1},{1,0},{2,3},{3,2},{4,5},{5,4},{6,7},{7,6},{8,9},{9,8},{10,11... | collective-permute-start | bytes 2359304 | tf_op jit(solution)/shard_map/ppermute | solution.py:700
  48.4 18.9 %collective-permute-start.4 = (bf16[256,1536]{1,0:T(8,128)(2,1)S(1)}, bf16[256,1536]{1,0:T(8,128)(2,1)}, u32[]{:S(2)}, u32[]{:S(2)}) collective-permute-start(bf16[256,1536]{1,0:T(8,128)(2,1)S(1)} %copy-done.2), channel_id=1, source_target_pairs={{0,2},{2,0},{1,3},{3,1},{4,6},{6,4},{5,7},{7,5},{8,10},{10,8},{9,1... | collective-permute-start | bytes 2359304 | tf_op jit(solution)/shard_map/ppermute | solution.py:700
  51.9 24.9 %collective-permute-start.3 = (bf16[256,1536]{1,0:T(8,128)(2,1)S(1)}, bf16[256,1536]{1,0:T(8,128)(2,1)S(1)}, u32[]{:S(2)}, u32[]{:S(2)}) collective-permute-start(bf16[256,1536]{1,0:T(8,128)(2,1)S(1)} %copy-done.2), channel_id=1, source_target_pairs={{0,1},{1,0},{2,3},{3,2},{4,5},{5,4},{6,7},{7,6},{8,9},{9,8},{10,11... | collective-permute-start | bytes 2359304 | tf_op jit(solution)/shard_map/ppermute | solution.py:700
  51.9 19.9 %collective-permute-start.2 = (bf16[256,1536]{1,0:T(8,128)(2,1)}, bf16[256,1536]{1,0:T(8,128)(2,1)S(1)}, u32[]{:S(2)}, u32[]{:S(2)}) collective-permute-start(bf16[256,1536]{1,0:T(8,128)(2,1)} %copy-done.6), channel_id=1, source_target_pairs={{0,1},{1,0},{2,3},{3,2},{4,5},{5,4},{6,7},{7,6},{8,9},{9,8},{10,11... | collective-permute-start | bytes 2359304 | tf_op jit(solution)/shard_map/ppermute | solution.py:700
  67.3 9.4 %collective-permute-start.5 = (bf16[256,1536]{1,0:T(8,128)(2,1)}, bf16[256,1536]{1,0:T(8,128)(2,1)S(1)}, u32[]{:S(2)}, u32[]{:S(2)}) collective-permute-start(bf16[256,1536]{1,0:T(8,128)(2,1)} %collective-permute-done.4.refs_2_), channel_id=1, source_target_pairs={{0,1},{1,0},{2,3},{3,2},{4,5},{5,4},{6,7},{7,6},{8,9},{9,8},{10,11... | collective-permute-start | bytes 2359304 | tf_op jit(solution)/shard_map/ppermute | solution.py:700
  122.6 5.4 %collective-permute-start.12 = (f32[8,1024]{1,0:T(8,128)S(1)}, f32[8,1024]{1,0:T(8,128)S(1)}, u32[]{:S(2)}, u32[]{:S(2)}) collective-permute-start(f32[8,1024]{1,0:T(8,128)S(1)} %add.179), channel_id=1, source_target_pairs={{0,2},{2,0},{1,3},{3,1},{4,6},{6,4},{5,7},{7,5},{8,10},{10,8},{9,1... | collective-permute-start | bytes 98312 | tf_op jit(solution)/shard_map/ppermute | solution.py:700
  148.7 50.7 %collective-permute-start.13 = (bf16[256,1536]{1,0:T(8,128)(2,1)}, bf16[256,1536]{1,0:T(8,128)(2,1)S(1)}, u32[]{:S(2)}, u32[]{:S(2)}) collective-permute-start(bf16[256,1536]{1,0:T(8,128)(2,1)} %get-tuple-element.103), channel_id=1, source_target_pairs={{0,1},{1,0},{2,3},{3,2},{4,5},{5,4},{6,7},{7,6},{8,9},{9,8},{10,11... | collective-permute-start | bytes 2359304 | tf_op jit(solution)/shard_map/ppermute | solution.py:700
  152.2 47.1 %collective-permute-start.15 = (bf16[256,1536]{1,0:T(8,128)(2,1)S(1)}, bf16[256,1536]{1,0:T(8,128)(2,1)S(1)}, u32[]{:S(2)}, u32[]{:S(2)}) collective-permute-start(bf16[256,1536]{1,0:T(8,128)(2,1)S(1)} %add_convert_fusion.1), channel_id=1, source_target_pairs={{0,2},{2,0},{1,3},{3,1},{4,6},{6,4},{5,7},{7,5},{8,10},{10,8},{9,1... | collective-permute-start | bytes 2359304 | tf_op jit(solution)/shard_map/ppermute | solution.py:700
  204.2 13.8 %collective-permute-start.21 = (bf16[416,512]{1,0:T(8,128)(2,1)}, bf16[416,512]{1,0:T(8,128)(2,1)S(1)}, u32[]{:S(2)}, u32[]{:S(2)}) collective-permute-start(bf16[416,512]{1,0:T(8,128)(2,1)} %get-tuple-element.138), channel_id=1, source_target_pairs={{0,24},{8,0},{16,8},{24,16},{1,25},{9,1},{17,9},{25,17},{2,26},{10... | collective-permute-start | bytes 1277960 | tf_op jit(solution)/shard_map/ppermute | solution.py:700
  205.1 15.6 %collective-permute-start.20 = (bf16[416,512]{1,0:T(8,128)(2,1)S(1)}, bf16[416,512]{1,0:T(8,128)(2,1)S(1)}, u32[]{:S(2)}, u32[]{:S(2)}) collective-permute-start(bf16[416,512]{1,0:T(8,128)(2,1)S(1)} %copy-done.39), channel_id=1, source_target_pairs={{0,8},{8,16},{16,24},{24,0},{1,9},{9,17},{17,25},{25,1},{2,10},{10... | collective-permute-start | bytes 1277960 | tf_op jit(solution)/shard_map/ppermute | solution.py:700
  206.2 16.8 %collective-permute-start.19 = (bf16[4,96,640]{2,1,0:T(8,128)(2,1)S(1)}, bf16[4,96,640]{2,1,0:T(8,128)(2,1)S(1)}, u32[]{:S(2)}, u32[]{:S(2)}) collective-permute-start(bf16[4,96,640]{2,1,0:T(8,128)(2,1)S(1)} %copy-done.37), channel_id=1, source_target_pairs={{0,96},{32,0},{64,32},{96,64},{1,97},{33,1},{65,33},{97,65},{2,98}... | collective-permute-start | bytes 1474568 | tf_op jit(solution)/shard_map/ppermute | solution.py:700
  207.1 28.2 %collective-permute-start.18 = (bf16[4,96,640]{2,1,0:T(8,128)(2,1)S(1)}, bf16[4,96,640]{2,1,0:T(8,128)(2,1)S(1)}, u32[]{:S(2)}, u32[]{:S(2)}) collective-permute-start(bf16[4,96,640]{2,1,0:T(8,128)(2,1)S(1)} %copy-done.36), channel_id=1, source_target_pairs={{0,64},{32,96},{64,0},{96,32},{1,65},{33,97},{65,1},{97,33},{2,66}... | collective-permute-start | bytes 1474568 | tf_op jit(solution)/shard_map/ppermute | solution.py:700
  208.9 27.1 %collective-permute-start.17 = (bf16[4,96,640]{2,1,0:T(8,128)(2,1)S(1)}, bf16[4,96,640]{2,1,0:T(8,128)(2,1)S(1)}, u32[]{:S(2)}, u32[]{:S(2)}) collective-permute-start(bf16[4,96,640]{2,1,0:T(8,128)(2,1)S(1)} %copy-done.35), channel_id=1, source_target_pairs={{0,32},{32,64},{64,96},{96,0},{1,33},{33,65},{65,97},{97,1},{2,34}... | collective-permute-start | bytes 1474568 | tf_op jit(solution)/shard_map/ppermute | solution.py:700
  220.7 15.3 %collective-permute-start.22 = (bf16[416,512]{1,0:T(8,128)(2,1)S(1)}, bf16[416,512]{1,0:T(8,128)(2,1)S(1)}, u32[]{:S(2)}, u32[]{:S(2)}) collective-permute-start(bf16[416,512]{1,0:T(8,128)(2,1)S(1)} %copy-done.38), channel_id=1, source_target_pairs={{0,16},{8,24},{16,0},{24,8},{1,17},{9,25},{17,1},{25,9},{2,18},{10... | collective-permute-start | bytes 1277960 | tf_op jit(solution)/shard_map/ppermute | solution.py:700
  221.4 29.9 %collective-permute-start.24 = (bf16[256,1536]{1,0:T(8,128)(2,1)}, bf16[256,1536]{1,0:T(8,128)(2,1)S(1)}, u32[]{:S(2)}, u32[]{:S(2)}) collective-permute-start(bf16[256,1536]{1,0:T(8,128)(2,1)} %add_convert_fusion), channel_id=1, source_target_pairs={{0,2},{2,0},{1,3},{3,1},{4,6},{6,4},{5,7},{7,5},{8,10},{10,8},{9,1... | collective-permute-start | bytes 2359304 | tf_op jit(solution)/shard_map/ppermute | solution.py:700
  240.8 11.3 %collective-permute-start.23 = (bf16[256,1536]{1,0:T(8,128)(2,1)}, bf16[256,1536]{1,0:T(8,128)(2,1)}, u32[]{:S(2)}, u32[]{:S(2)}) collective-permute-start(bf16[256,1536]{1,0:T(8,128)(2,1)} %get-tuple-element.144), channel_id=1, source_target_pairs={{0,1},{1,0},{2,3},{3,2},{4,5},{5,4},{6,7},{7,6},{8,9},{9,8},{10,11... | collective-permute-start | bytes 2359304 | tf_op jit(solution)/shard_map/ppermute | solution.py:700
  240.9 7.3 %collective-permute-start.29 = (bf16[128,512]{1,0:T(8,128)(2,1)}, bf16[128,512]{1,0:T(8,128)(2,1)S(1)}, u32[]{:S(2)}, u32[]{:S(2)}) collective-permute-start(bf16[128,512]{1,0:T(8,128)(2,1)} %get-tuple-element.154), channel_id=1, source_target_pairs={{0,96},{32,0},{64,32},{96,64},{1,97},{33,1},{65,33},{97,65},{2,98}... | collective-permute-start | bytes 393224 | tf_op jit(solution)/shard_map/ppermute | solution.py:700
  241.7 8.1 %collective-permute-start.28 = (bf16[128,512]{1,0:T(8,128)(2,1)}, bf16[128,512]{1,0:T(8,128)(2,1)S(1)}, u32[]{:S(2)}, u32[]{:S(2)}) collective-permute-start(bf16[128,512]{1,0:T(8,128)(2,1)} %get-tuple-element.151), channel_id=1, source_target_pairs={{0,32},{32,64},{64,96},{96,0},{1,33},{33,65},{65,97},{97,1},{2,34}... | collective-permute-start | bytes 393224 | tf_op jit(solution)/shard_map/ppermute | solution.py:700
  244.2 15.5 %collective-permute-start.27 = (bf16[96,640]{1,0:T(8,128)(2,1)}, bf16[96,640]{1,0:T(8,128)(2,1)}, u32[]{:S(2)}, u32[]{:S(2)}) collective-permute-start(bf16[96,640]{1,0:T(8,128)(2,1)} %get-tuple-element.143), channel_id=1, source_target_pairs={{0,24},{8,0},{16,8},{24,16},{1,25},{9,1},{17,9},{25,17},{2,26},{10... | collective-permute-start | bytes 368648 | tf_op jit(solution)/shard_map/ppermute | solution.py:700
  248.2 11.4 %collective-permute-start.26 = (bf16[96,640]{1,0:T(8,128)(2,1)}, bf16[96,640]{1,0:T(8,128)(2,1)}, u32[]{:S(2)}, u32[]{:S(2)}) collective-permute-start(bf16[96,640]{1,0:T(8,128)(2,1)} %get-tuple-element.142), channel_id=1, source_target_pairs={{0,16},{8,24},{16,0},{24,8},{1,17},{9,25},{17,1},{25,9},{2,18},{10... | collective-permute-start | bytes 368648 | tf_op jit(solution)/shard_map/ppermute | solution.py:700
  249.7 9.9 %collective-permute-start.25 = (bf16[96,640]{1,0:T(8,128)(2,1)}, bf16[96,640]{1,0:T(8,128)(2,1)}, u32[]{:S(2)}, u32[]{:S(2)}) collective-permute-start(bf16[96,640]{1,0:T(8,128)(2,1)} %get-tuple-element.141), channel_id=1, source_target_pairs={{0,8},{8,16},{16,24},{24,0},{1,9},{9,17},{17,25},{25,1},{2,10},{10... | collective-permute-start | bytes 368648 | tf_op jit(solution)/shard_map/ppermute | solution.py:700
  251.3 8.3 %collective-permute-start.30 = (bf16[128,512]{1,0:T(8,128)(2,1)}, bf16[128,512]{1,0:T(8,128)(2,1)S(1)}, u32[]{:S(2)}, u32[]{:S(2)}) collective-permute-start(bf16[128,512]{1,0:T(8,128)(2,1)} %get-tuple-element.155), channel_id=1, source_target_pairs={{0,64},{32,96},{64,0},{96,32},{1,65},{33,97},{65,1},{97,33},{2,66}... | collective-permute-start | bytes 393224 | tf_op jit(solution)/shard_map/ppermute | solution.py:700
  254.7 9.1 %collective-permute-start.35 = (bf16[48,1536]{1,0:T(8,128)(2,1)S(1)}, bf16[48,1536]{1,0:T(8,128)(2,1)S(1)}, u32[]{:S(2)}, u32[]{:S(2)}) collective-permute-start(bf16[48,1536]{1,0:T(8,128)(2,1)S(1)} %dynamic-slice_bitcast_fusion), channel_id=1, source_target_pairs={{0,4},{4,0},{1,5},{5,1},{2,6},{6,2},{3,7},{7,3},{8,12},{12,8},{9,1... | collective-permute-start | bytes 442376 | tf_op jit(solution)/shard_map/ppermute | solution.py:700
  262.5 5.7 %collective-permute-start.31 = (bf16[80,1152]{1,0:T(8,128)(2,1)}, bf16[80,1152]{1,0:T(8,128)(2,1)S(1)}, u32[]{:S(2)}, u32[]{:S(2)}) collective-permute-start(bf16[80,1152]{1,0:T(8,128)(2,1)} %get-tuple-element.159), channel_id=1, source_target_pairs={{0,4},{4,0},{1,5},{5,1},{2,6},{6,2},{3,7},{7,3},{8,12},{12,8},{9,1... | collective-permute-start | bytes 552968 | tf_op jit(solution)/shard_map/ppermute | solution.py:700
  271.7 6.0 %collective-permute-start.33 = (f32[28,512]{1,0:T(8,128)S(1)}, f32[28,512]{1,0:T(8,128)S(1)}, u32[]{:S(2)}, u32[]{:S(2)}) collective-permute-start(f32[28,512]{1,0:T(8,128)S(1)} %get-tuple-element.231), channel_id=1, source_target_pairs={{0,2},{1,3},{2,0},{3,1},{4,6},{5,7},{6,4},{7,5},{8,10},{9,11},{10,... | collective-permute-start | bytes 172040 | tf_op jit(solution)/shard_map/ppermute | solution.py:718
  273.6 5.6 %collective-permute-start.34 = (f32[28,512]{1,0:T(8,128)S(1)}, f32[28,512]{1,0:T(8,128)S(1)}, u32[]{:S(2)}, u32[]{:S(2)}) collective-permute-start(f32[28,512]{1,0:T(8,128)S(1)} %get-tuple-element.229), channel_id=1, source_target_pairs={{0,3},{1,2},{2,1},{3,0},{4,7},{5,6},{6,5},{7,4},{8,11},{9,10},{10,... | collective-permute-start | bytes 172040 | tf_op jit(solution)/shard_map/ppermute | solution.py:718
  (47 other events, 538.2 us)
Sparse Core Ops, SparseCore 0:
  27.6 68.6 all-gather.1
  147.7 89.5 reduce-scatter.1
